TPU v7x, 512 devices: a whole 4x4x16 slice. The times are simulated.
512 devices in a mesh: row: 16 (over x, y), col: 32 (over z, core).
Axes of the slice: x: 4, y: 4, z: 16, core: 2. Of those that a mesh axis runs over, the one named last changes fastest.
Arguments:
- diag_tile: bfloat16 [1024, 1024], P('row'), as said below
- row_u: bfloat16 [16, 1024, 256], P('row', 'col'), may hold values from -6 to 6
- row_v: bfloat16 [16, 1024, 256], P('row', 'col'), may hold values from -0.1875 to 0.1875
- col_u: bfloat16 [32, 1024, 256], P('col', 'row'), may hold values from -6 to 6
- col_v: bfloat16 [32, 1024, 256], P('col', 'row'), may hold values from -0.1875 to 0.1875
- tile_u: bfloat16 [16, 32, 1024, 256], P('row', 'col'), may hold values from -6 to 6
- tile_v: bfloat16 [16, 32, 1024, 256], P('row', 'col'), may hold values from -0.375 to 0.375
- omega: bfloat16 [1024, 128], replicated, may hold values from -6 to 6
- row_rank: int32 [16], P('row'), may hold values from 96 to 256, as said below
- col_rank: int32 [32], P('col'), may hold values from 96 to 256, as said below
- tile_rank: int32 [16, 32], P('row', 'col'), may hold values from 96 to 256, as said below
- keep_rank: int32 [16, 32], P('row', 'col'), may hold values from 32 to 128, as said below
Outputs:
- diag_factor: float32 [1024, 1024], P('row')
- row_solved: bfloat16 [16, 1024, 256], P('row', 'col')
- col_solved: bfloat16 [32, 1024, 256], P('col', 'row')
- new_u: bfloat16 [16, 32, 1024, 128], P('row', 'col')
- new_v: bfloat16 [16, 32, 1024, 128], P('row', 'col')
Inputs may be any that keep to these rules, and one draw needn't show every extreme that they name: `row_rank`: columns of a panel factor at or past its rank hold arbitrary values; some tile has rank exactly 256. `col_rank`: as for row_rank. `tile_rank`: as for row_rank. `keep_rank`: some tile keeps exactly 128. `diag_tile`: symmetric positive definite covariance tile.
All inputs are finite; a program needn't handle non-finite values.
Results may differ from a plain program's by a relative error of at most 0.011.
Values may be sent and summed in bfloat16 or wider, within the bound.
No kernel may reach another device: no remote copies, remote signals or barrier semaphores. Data moves between devices by JAX's collectives and lax.ppermute only.
A program may use at most 128 MiB of HBM per device.

v0:
```python
import jax
import jax.numpy as jnp
from jax import lax
from jax.sharding import PartitionSpec as P

HIGH = lax.Precision.HIGHEST


def cut_columns(values, ranks):
    width = values.shape[-1]
    live = jnp.arange(width, dtype=jnp.int32) < ranks[..., None, None]
    return jnp.where(live, values, jnp.zeros_like(values))


def recompress(tu, tv, trank, krank, u_row, couple, u_col, omega):
    width = tu.shape[-1]
    keep = omega.shape[-1]
    live = (jnp.arange(width, dtype=jnp.int32) < trank)[None, :]
    u_tile = jnp.where(live, tu, jnp.zeros_like(tu)).astype(jnp.float32)
    v_tile = jnp.where(live, tv, jnp.zeros_like(tv)).astype(jnp.float32)
    row_f = u_row.astype(jnp.float32)
    col_f = u_col.astype(jnp.float32)
    kept = jnp.arange(keep, dtype=jnp.int32) < krank
    sketch = jnp.where(kept[None, :], omega.astype(jnp.float32), jnp.float32(0.0))
    inner_top = jnp.einsum("nk,nr->kr", v_tile, sketch, precision=HIGH)
    inner_low = -jnp.einsum("nk,nr->kr", col_f, sketch, precision=HIGH)
    mixed = jnp.dot(couple, inner_low, precision=HIGH)
    sample = jnp.dot(u_tile, inner_top, precision=HIGH) + jnp.dot(row_f, mixed, precision=HIGH)
    gram = jnp.einsum("nr,ns->rs", sample, sample, precision=HIGH)
    gram = gram + jnp.diag(jnp.where(kept, jnp.float32(0.0), jnp.float32(1.0)))
    lower = jnp.linalg.cholesky(gram)
    basis_t = lax.linalg.triangular_solve(lower, sample.T, left_side=True, lower=True)
    basis = basis_t.T
    proj_top = jnp.einsum("nk,nr->kr", u_tile, basis, precision=HIGH)
    row_proj = jnp.einsum("nk,nr->kr", row_f, basis, precision=HIGH)
    proj_low = jnp.einsum("pk,pr->kr", couple, row_proj, precision=HIGH)
    weights = jnp.dot(v_tile, proj_top, precision=HIGH) - jnp.dot(col_f, proj_low, precision=HIGH)
    scale = jnp.float32(tu.shape[0]) ** 0.5
    return ((basis * scale).astype(jnp.bfloat16), weights.astype(jnp.bfloat16))


def solve_whole(inverse, factors):
    return jnp.einsum("mn,ank->amk", inverse, factors, preferred_element_type=jnp.float32).astype(
        jnp.bfloat16
    )


def per_device(
    diag_tile,
    row_u,
    row_v,
    col_u,
    col_v,
    tile_u,
    tile_v,
    omega,
    row_rank,
    col_rank,
    tile_rank,
    keep_rank,
):
    ru = cut_columns(row_u, row_rank)
    rv = cut_columns(row_v, row_rank)
    cu = cut_columns(col_u, col_rank)
    cv = cut_columns(col_v, col_rank)
    ru_full, rv_full = (
        lax.all_gather(ru, "col", axis=1, tiled=True),
        lax.all_gather(rv, "col", axis=1, tiled=True),
    )
    cu_full, cv_full = (
        lax.all_gather(cu, "row", axis=1, tiled=True),
        lax.all_gather(cv, "row", axis=1, tiled=True),
    )
    diag_rows = diag_tile.shape[0]
    order = diag_tile.shape[1]
    whole = lax.all_gather(diag_tile, "row", axis=0, tiled=True)
    factor = jnp.linalg.cholesky(whole.astype(jnp.float32))
    inverse = lax.linalg.triangular_solve(
        factor, jnp.eye(order, dtype=jnp.float32), left_side=True, lower=True
    )
    inverse = inverse.astype(jnp.bfloat16)
    diag_out = lax.dynamic_slice_in_dim(factor, lax.axis_index("row") * diag_rows, diag_rows, 0)
    row_here = ru.shape[1]
    col_here = cu.shape[1]
    rw_full = solve_whole(inverse, rv_full)
    row_out = lax.dynamic_slice_in_dim(rw_full, lax.axis_index("col") * row_here, row_here, 1)
    cw_full = solve_whole(inverse, cv_full)
    col_out = lax.dynamic_slice_in_dim(cw_full, lax.axis_index("row") * col_here, col_here, 1)
    couple = jnp.einsum("anp,bnq->abpq", rw_full, cw_full, preferred_element_type=jnp.float32)
    across = jax.vmap(recompress, in_axes=(0, 0, 0, 0, None, 0, 0, None))
    downward = jax.vmap(across, in_axes=(0, 0, 0, 0, 0, 0, None, None))
    new_u, new_v = downward(tile_u, tile_v, tile_rank, keep_rank, ru_full, couple, cu_full, omega)
    return (diag_out, row_out, col_out, new_u, new_v)


def solution(mesh):
    return jax.shard_map(
        per_device,
        mesh=mesh,
        in_specs=(
            P("row", None),
            P("row", "col", None),
            P("row", "col", None),
            P("col", "row", None),
            P("col", "row", None),
            P("row", "col", None, None),
            P("row", "col", None, None),
            P(),
            P("row"),
            P("col"),
            P("row", "col"),
            P("row", "col"),
        ),
        out_specs=(
            P("row", None),
            P("row", "col", None),
            P("col", "row", None),
            P("row", "col", None, None),
            P("row", "col", None, None),
        ),
        check_vma=False,
    )
```

profile of v0, /device:TPU:1, one launch (start us, length us, event | category | flops | bytes accessed | tf_op | source)
XLA Modules:
  0.0 539.6 jit_solution(4063667627672135962)
XLA Ops:
  11.4 21.9 %all_gather.17 = bf16[1,1024,256]{2,1,0:T(8,128)(2,1)} all-gather(bf16[1,64,256]{2,1,0:T(8,128)(2,1)S(1)} %get-tuple-element.74), channel_id=1, replica_groups=mesh['row'=16,'col'=32] {'row'}, dimensions={1}, use_global_device_ids=true | all-gather | bytes 557056 | tf_op jit(solution)/shard_map/all_gather | solution.py:72
  33.3 18.8 %all_gather.19 = bf16[1,1024,256]{2,1,0:T(8,128)(2,1)S(1)} all-gather(bf16[1,64,256]{2,1,0:T(8,128)(2,1)S(1)} %get-tuple-element.73), channel_id=1, replica_groups=mesh['row'=16,'col'=32] {'row'}, dimensions={1}, use_global_device_ids=true | all-gather | bytes 557056 | tf_op jit(solution)/shard_map/all_gather | solution.py:71
  52.1 1.3 iota_compare_fusion
  53.4 2.4 fusion.25
  57.3 1.4 fusion.51
  58.7 51.8 %all_gather.16 = bf16[1,1024,256]{2,1,0:T(8,128)(2,1)} all-gather(bf16[1,32,256]{2,1,0:T(8,128)(2,1)S(1)} %get-tuple-element.72), channel_id=1, replica_groups=mesh['row'=16,'col'=32] {'col'}, dimensions={1}, use_global_device_ids=true | all-gather | bytes 540672 | tf_op jit(solution)/shard_map/all_gather | solution.py:68
  110.5 28.5 %all_gather.18 = bf16[1,1024,256]{2,1,0:T(8,128)(2,1)S(1)} all-gather(bf16[1,32,256]{2,1,0:T(8,128)(2,1)S(1)} %get-tuple-element.71), channel_id=1, replica_groups=mesh['row'=16,'col'=32] {'col'}, dimensions={1}, use_global_device_ids=true | all-gather | bytes 540672 | tf_op jit(solution)/shard_map/all_gather | solution.py:67
  139.0 2.9 copy.73
  141.9 3.5 copy.74
  145.4 2.9 fusion
  148.3 2.0 copy-done.1
  150.3 11.7 %cholesky.246 = f32[128,128]{1,0:T(8,128)S(1)} custom-call(f32[128,128]{1,0:T(8,128)S(1)} %cholesky.640), custom_call_target="Cholesky" | custom-call | tf_op jit(solution)/shard_map/jit(cholesky)/cholesky | solution.py:77
  162.1 2.5 cholesky.276
  164.8 9.8 %custom-call.69 = f32[1,128,128]{1,2,0:T(8,128)S(1)} custom-call(f32[1,128,128]{2,1,0:T(8,128)S(1)} %copy.77), custom_call_target="InvertDiagBlocksLowerTriangular" | custom-call | tf_op jit(solution)/shard_map/jit(cholesky)/cholesky | solution.py:77
  174.7 2.4 constant_dynamic-update-slice_fusion.23
  177.0 1.5 convolution_subtract_fusion.6
  178.6 11.7 %cholesky.269 = f32[128,128]{1,0:T(8,128)S(1)} custom-call(f32[128,128]{1,0:T(8,128)S(1)} %cholesky.644), custom_call_target="Cholesky" | custom-call | tf_op jit(solution)/shard_map/jit(cholesky)/cholesky | solution.py:77
  191.3 10.0 %custom-call.70 = f32[1,128,128]{1,2,0:T(8,128)S(1)} custom-call(f32[1,128,128]{2,1,0:T(8,128)S(1)} %copy.80), custom_call_target="InvertDiagBlocksLowerTriangular" | custom-call | tf_op jit(solution)/shard_map/jit(cholesky)/cholesky | solution.py:77
  201.3 1.2 convolution_dynamic-update-slice_fusion
  202.5 2.1 convolution_subtract_fusion.7
  204.6 11.7 %cholesky.514 = f32[128,128]{1,0:T(8,128)S(1)} custom-call(f32[128,128]{1,0:T(8,128)S(1)} %cholesky.649), custom_call_target="Cholesky" | custom-call | tf_op jit(solution)/shard_map/jit(cholesky)/cholesky | solution.py:77
  217.3 9.8 %custom-call.71 = f32[1,128,128]{1,2,0:T(8,128)S(1)} custom-call(f32[1,128,128]{2,1,0:T(8,128)S(1)} %copy.83), custom_call_target="InvertDiagBlocksLowerTriangular" | custom-call | tf_op jit(solution)/shard_map/jit(cholesky)/cholesky | solution.py:77
  227.1 1.2 convolution_dynamic-update-slice_fusion.1
  228.3 2.3 convolution_subtract_fusion.8
  230.6 11.9 %cholesky.533 = f32[128,128]{1,0:T(8,128)S(1)} custom-call(f32[128,128]{1,0:T(8,128)S(1)} %cholesky.654), custom_call_target="Cholesky" | custom-call | tf_op jit(solution)/shard_map/jit(cholesky)/cholesky | solution.py:77
  243.5 9.8 %custom-call.72 = f32[1,128,128]{1,2,0:T(8,128)S(1)} custom-call(f32[1,128,128]{2,1,0:T(8,128)S(1)} %copy.86), custom_call_target="InvertDiagBlocksLowerTriangular" | custom-call | tf_op jit(solution)/shard_map/jit(cholesky)/cholesky | solution.py:77
  253.3 1.1 convolution_dynamic-update-slice_fusion.2
  254.4 2.3 convolution_subtract_fusion.9
  256.8 11.7 %cholesky.552 = f32[128,128]{1,0:T(8,128)S(1)} custom-call(f32[128,128]{1,0:T(8,128)S(1)} %cholesky.659), custom_call_target="Cholesky" | custom-call | tf_op jit(solution)/shard_map/jit(cholesky)/cholesky | solution.py:77
  269.5 10.2 %custom-call.73 = f32[1,128,128]{1,2,0:T(8,128)S(1)} custom-call(f32[1,128,128]{2,1,0:T(8,128)S(1)} %copy.89), custom_call_target="InvertDiagBlocksLowerTriangular" | custom-call | tf_op jit(solution)/shard_map/jit(cholesky)/cholesky | solution.py:77
  279.6 1.0 convolution_dynamic-update-slice_fusion.3
  280.7 2.3 convolution_subtract_fusion.10
  283.0 11.7 %cholesky.572 = f32[128,128]{1,0:T(8,128)S(1)} custom-call(f32[128,128]{1,0:T(8,128)S(1)} %cholesky.664), custom_call_target="Cholesky" | custom-call | tf_op jit(solution)/shard_map/jit(cholesky)/cholesky | solution.py:77
  295.6 9.8 %custom-call.74 = f32[1,128,128]{1,2,0:T(8,128)S(1)} custom-call(f32[1,128,128]{2,1,0:T(8,128)S(1)} %copy.92), custom_call_target="InvertDiagBlocksLowerTriangular" | custom-call | tf_op jit(solution)/shard_map/jit(cholesky)/cholesky | solution.py:77
  306.4 2.0 convolution_subtract_fusion.11
  308.4 11.8 %cholesky.592 = f32[128,128]{1,0:T(8,128)S(1)} custom-call(f32[128,128]{1,0:T(8,128)S(1)} %cholesky.669), custom_call_target="Cholesky" | custom-call | tf_op jit(solution)/shard_map/jit(cholesky)/cholesky | solution.py:77
  321.2 9.8 %custom-call.75 = f32[1,128,128]{1,2,0:T(8,128)S(1)} custom-call(f32[1,128,128]{2,1,0:T(8,128)S(1)} %copy.95), custom_call_target="InvertDiagBlocksLowerTriangular" | custom-call | tf_op jit(solution)/shard_map/jit(cholesky)/cholesky | solution.py:77
  331.8 1.8 convolution_subtract_fusion.12
  333.6 11.7 %cholesky.610 = f32[128,128]{1,0:T(8,128)S(1)} custom-call(f32[128,128]{1,0:T(8,128)S(1)} %convolution_subtract_fusion.12), custom_call_target="Cholesky" | custom-call | tf_op jit(solution)/shard_map/jit(cholesky)/cholesky | solution.py:77
  355.9 6.7 %fusion.1 = (f32[1024,1024]{1,0:T(8,128)}, f32[1024,1024]{1,0:T(8,128)}) fusion(f32[1024,1024]{1,0:T(8,128)} %constant_dynamic-update-slice_fusion.24, pred[]{:T(512)S(6)} %cholesky.639), kind=kLoop, calls=%fused_computation.7 | loop fusion | flops 4194304 | bytes 12582913 | tf_op jit(solution)/shard_map/triangular_solve | solution.py:78
  362.6 28.0 %while.1 = (s32[]{:T(128)}, f32[1024,1024]{1,0:T(8,128)}, s32[8,2]{0,1:T(2,128)S(1)}, f32[8,128,128]{2,1,0:T(8,128)}, s32[]{:T(128)}) while((s32[]{:T(128)}, f32[1024,1024]{1,0:T(8,128)}, s32[8,2]{0,1:T(2,128)S(1)}, f32[8,128,128]{2,1,0:T(8,128)}, s32[]{:T(128)}) %tuple.57), condition=%wide.while_cond, body=%wide.while_body.sunk | while | flops 2 | bytes 132205 | solution.py:78
  363.2 2.9 bitcast_dynamic-update-slice_fusion.2
  366.7 2.9 bitcast_dynamic-update-slice_fusion.2
  370.2 2.9 bitcast_dynamic-update-slice_fusion.2
  373.7 2.9 bitcast_dynamic-update-slice_fusion.2
  377.2 2.9 bitcast_dynamic-update-slice_fusion.2
  380.7 2.9 bitcast_dynamic-update-slice_fusion.2
  384.2 2.9 bitcast_dynamic-update-slice_fusion.2
  387.7 2.8 bitcast_dynamic-update-slice_fusion.2
  390.6 79.6 %custom-call.76 = f32[8,128,128]{1,2,0:T(8,128)S(1)} custom-call(f32[8,128,128]{2,1,0:T(8,128)} %get-tuple-element.12), custom_call_target="InvertDiagBlocksLowerTriangular" | custom-call | tf_op jit(solution)/shard_map/triangular_solve | solution.py:78
  470.2 1.4 convert_dynamic-update-slice_fusion.6
  471.8 1.7 convolution_subtract_fusion.4
  474.1 1.6 convolution_subtract_fusion
  476.4 2.0 fusion.16
  479.1 2.2 fusion.19
  482.7 2.6 convolution_subtract_fusion.2
  486.1 2.8 convolution_subtract_fusion.1
  489.7 3.7 convolution_subtract_fusion.3
  497.2 1.0 convolution_add_fusion.1
  498.4 11.7 %custom-call.77 = f32[1,1,128,128]{3,2,1,0:T(8,128)S(1)} custom-call(f32[1,1,128,128]{3,2,1,0:T(8,128)S(1)} %fusion.94), custom_call_target="Cholesky" | custom-call | tf_op jit(solution)/shard_map/vmap(vmap(jit(cholesky)))/cholesky | solution.py:31
  511.4 9.8 %custom-call.78 = f32[1,1,1,128,128]{3,4,2,1,0:T(8,128)S(1)} custom-call(f32[1,1,1,128,128]{4,3,2,1,0:T(8,128)S(1)} %fusion.84), custom_call_target="InvertDiagBlocksLowerTriangular" | custom-call | tf_op jit(solution)/shard_map/vmap(vmap())/triangular_solve | solution.py:32
  524.4 1.7 constant_dynamic-slice_fusion.3
  529.3 1.6 fusion.45
  531.3 1.3 fusion.24
  (135 shorter events, 37.6 us)
Async XLA Ops:
  7.2 48.7 %copy-start.11 = (bf16[1,32,256]{2,1,0:T(8,128)(2,1)S(1)}, bf16[1,32,256]{2,1,0:T(8,128)(2,1)}, u32[]{:S(2)}) copy-start(bf16[1,32,256]{2,1,0:T(8,128)(2,1)} %param.13) | copy-start | bytes 49156
  7.2 48.7 %copy-start.12 = (bf16[1,32,256]{2,1,0:T(8,128)(2,1)S(1)}, bf16[1,32,256]{2,1,0:T(8,128)(2,1)}, u32[]{:S(2)}) copy-start(bf16[1,32,256]{2,1,0:T(8,128)(2,1)} %param.14) | copy-start | bytes 49156
  7.2 48.7 %copy-start.10 = (bf16[1024,128]{1,0:T(8,128)(2,1)S(1)}, bf16[1024,128]{1,0:T(8,128)(2,1)}, u32[]{:S(2)}) copy-start(bf16[1024,128]{1,0:T(8,128)(2,1)} %param.19) | copy-start | bytes 786436
  7.2 49.4 %copy-start.7 = (bf16[1,1,1024,256]{3,2,1,0:T(8,128)(2,1)S(1)}, bf16[1,1,1024,256]{3,2,1,0:T(8,128)(2,1)}, u32[]{:S(2)}) copy-start(bf16[1,1,1024,256]{3,2,1,0:T(8,128)(2,1)} %param.18) | copy-start | bytes 1572868
  7.2 131.8 %all-gather.2.cloned.1.call-start = ((), (), s32[]{:S(2)}) async-start(), calls=%async_computation | async-start | bytes 2228224 | tf_op jit(solution)/shard_map/all_gather | solution.py:76
  33.3 24.0 %copy-start.2 = (bf16[1,1,1024,256]{3,2,1,0:T(8,128)(2,1)S(1)}, bf16[1,1,1024,256]{3,2,1,0:T(8,128)(2,1)}, u32[]{:S(2)}) copy-start(bf16[1,1,1024,256]{3,2,1,0:T(8,128)(2,1)} %param.17) | copy-start | bytes 1572868
  148.3 2.0 copy-start.1
  470.2 3.9 copy-start
  489.0 5.1 copy-start.9
  489.7 5.2 copy-start.8
  494.1 2.6 copy-start.4
  494.9 2.4 copy-start.5
  494.9 27.2 %copy-start.3 = (bf16[1,1,1024,256]{3,2,1,0:T(8,128)(2,1)S(1)}, bf16[1,1,1024,256]{3,2,1,0:T(8,128)(2,1)}, u32[]{:S(2)}) copy-start(bf16[1,1,1024,256]{3,2,1,0:T(8,128)(2,1)} %param.17) | copy-start | bytes 1572868
  495.7 2.6 copy-start.6
Sparse Core Ops, SparseCore 0:
  11.1 64.7 all-gather.1
where the time goes:
time: 545 us; the launch traced here: 540 us
  other arithmetic  285 us (52%)
  blocking collectives  121 us (22%)
  matrix products  58.1 us (11%)
  local copies, waits for them, and re-layouts  51.8 us (10%)
  between operations  22.8 us (4%)
    another operation x30, other arithmetic, per_device(): factor = jnp.linalg.cholesky(whole.astype(jnp.float32))  169 us
    another operation x3, other arithmetic, per_device(): lax.linalg.triangular_solve(factor, jnp.eye(order, dtype=jnp.float32), le...  86.3 us
    all_gather x1, blocking collectives, per_device(): lax.all_gather(rv, 'col', axis=1, tiled=True)  51.8 us
    another operation x28, local copies, waits for them, and re-layouts  31.3 us
    all_gather x1, blocking collectives, per_device(): lax.all_gather(ru, 'col', axis=1, tiled=True)  28.5 us
    another operation x14, matrix products, per_device(): factor = jnp.linalg.cholesky(whole.astype(jnp.float32))  23.1 us
    another operation x15, matrix products, per_device(): lax.linalg.triangular_solve(factor, jnp.eye(order, dtype=jnp.float32), le...  22.6 us
    all_gather x1, blocking collectives, per_device(): lax.all_gather(cv, 'row', axis=1, tiled=True)  21.9 us
  transfers between devices with their start and end apart: 1, of which 0 were waited for; matrix products, arithmetic and copies ran while one was open for 1% of the time, Pallas kernels for 0%

commit v1 on v0

v1 whole, which is shorter than its diff:
```python
import jax, jax.numpy as jnp
from jax import lax
from jax.sharding import PartitionSpec as P
from jax.experimental import pallas as pl
from jax.experimental.pallas import tpu as pltpu
F32=jnp.float32; BF=jnp.bfloat16
G=8

def lane(x,c): return jnp.broadcast_to(x[:,c:c+1],(8,128))
def sub(x,s): return jnp.broadcast_to(x[s:s+1,:],(8,128))

def factor(S):
    row=lax.broadcasted_iota(jnp.int32,(8,128),0); col=lax.broadcasted_iota(jnp.int32,(8,128),1)
    W=[jnp.where(col==row+8*g,F32(1),F32(0)) for g in range(16)]
    S=list(S)
    for p in range(16):
        C={g:[lane(S[g],8*p+j) for j in range(8)] for g in range(p,16)}
        a=[[sub(C[p][j],i) if i>=j else None for j in range(8)] for i in range(8)]
        B=[sub(S[p],j) for j in range(8)]; V=[sub(W[p],j) for j in range(8)]
        r=[None]*8
        l=[[None]*8 for _ in range(8)]
        for j in range(8):
            r[j]=lax.rsqrt(a[j][j])
            for i in range(j+1,8): l[i][j]=a[i][j]*r[j]
            B[j]=B[j]*r[j]; V[j]=V[j]*r[j]
            for i in range(j+1,8):
                for k in range(j+1,i+1): a[i][k]=a[i][k]-l[i][j]*l[k][j]
                B[i]=B[i]-l[i][j]*B[j]; V[i]=V[i]-l[i][j]*V[j]
        S[p]=B[0]; W[p]=V[0]
        for j in range(1,8):
            S[p]=jnp.where(row==j,B[j],S[p]); W[p]=jnp.where(row==j,V[j],W[p])
        if p<15:
            X=list(B); Y=list(V)
            for j in range(7,-1,-1):
                X[j]=X[j]*r[j]; Y[j]=Y[j]*r[j]
                for i in range(j):
                    X[i]=X[i]-l[j][i]*X[j]; Y[i]=Y[i]-l[j][i]*Y[j]
            for g in range(p+1,16):
                t=[C[g][j]*X[j] for j in range(8)]; u=[C[g][j]*Y[j] for j in range(8)]
                S[g]=S[g]-(((t[0]+t[1])+(t[2]+t[3]))+((t[4]+t[5])+(t[6]+t[7])))
                W[g]=W[g]-(((u[0]+u[1])+(u[2]+u[3]))+((u[4]+u[5])+(u[6]+u[7])))
    return S,W

def split(x):
    h=x.astype(BF); return h,(x-h.astype(F32)).astype(BF)
def dotg(a,b,ca,cb): return lax.dot_general(a,b,(((ca,),(cb,)),((),())),preferred_element_type=F32)
def dot3(a,b,ca,cb):
    ah,al=split(a); bh,bl=split(b)
    return dotg(ah,bh,ca,cb)+(dotg(ah,bl,ca,cb)+dotg(al,bh,ca,cb))

def chol_kernel(who,mine,other,l_ref,m_ref,buf,lcol):
    N=1024; nb=8
    strip=who[0]; b=lax.shift_right_logical(strip,1)
    c=lax.bitwise_and(who[1],1)*32
    for s in range(16):
        buf[pl.ds(pl.multiple_of(64*s+c,32),32),:]=mine[s].astype(F32)
        buf[pl.ds(pl.multiple_of(64*s+32-c,32),32),:]=other[s].astype(F32)
    l_ref[...]=jnp.zeros_like(l_ref)
    m_ref[...]=jnp.zeros_like(m_ref)
    def step(k,_):
        k0=pl.multiple_of(k*128,128)
        blk=pl.ds(k0,128)
        S,W=factor([buf[pl.ds(pl.multiple_of(k0+8*g,8),8),blk] for g in range(16)])
        row=lax.broadcasted_iota(jnp.int32,(8,128),0); col=lax.broadcasted_iota(jnp.int32,(8,128),1)
        R=jnp.concatenate([jnp.where(col>=row+8*g,S[g],F32(0)) for g in range(16)],0)
        M=jnp.concatenate(W,0)
        @pl.when(k==b)
        def _():
            lcol[pl.ds(0,128),:]=R.T
            l_ref[:,blk]=lcol[pl.ds(pl.multiple_of((lax.bitwise_and(strip,1))*64,64),64),:]
        mh,ml=split(M)
        pan=buf[blk,:]
        ph,plo=split(pan)
        pan=dotg(mh,ph,1,0)+(dotg(mh,plo,1,0)+dotg(ml,ph,1,0))
        buf[blk,:]=pan
        buf[blk,blk]=M
        for kk in range(nb-1):
            @pl.when(k==kk)
            def _():
                n0=128*(kk+1)
                low=buf[n0:,kk*128:kk*128+128]
                lh,ll=split(low)
                lc=dotg(lh,mh,1,1)+(dotg(lh,ml,1,1)+dotg(ll,mh,1,1))
                lcol[n0:,:]=lc
                ch,cl=split(lc)
                lhs=jnp.concatenate([ch,cl,ch],1)
                qh,ql=split(buf[kk*128:kk*128+128,:])
                rhs=jnp.concatenate([qh,qh,ql],0)
                buf[n0:,kk*128:kk*128+128]=jnp.zeros((N-n0,128),F32)
                buf[n0:,:]=buf[n0:,:]-dotg(lhs,rhs,1,0)
        @pl.when(k<b)
        def _():
            l_ref[:,blk]=lcol[pl.ds(pl.multiple_of(strip*64,64),64),:]
        return 0
    lax.fori_loop(0,nb,step,0)
    for k in range(nb):
        n1=128*(k+1)
        m_ref[k*128:n1,:n1]=buf[k*128:n1,:n1].astype(BF)

def chol(who,mine,other):
    return pl.pallas_call(chol_kernel,
        out_shape=(jax.ShapeDtypeStruct((64,1024),F32),jax.ShapeDtypeStruct((1024,1024),BF)),
        in_specs=[pl.BlockSpec(memory_space=pltpu.SMEM)]+[pl.BlockSpec(memory_space=pltpu.VMEM)]*2,
        out_specs=(pl.BlockSpec(memory_space=pltpu.VMEM),)*2,
        scratch_shapes=[pltpu.VMEM((1024,1024),F32),pltpu.VMEM((1024,128),F32)],
        compiler_params=pltpu.CompilerParams(vmem_limit_bytes=18*2**20),
        name="chol_inverse",cost_estimate=pl.CostEstimate(flops=3*10**10,bytes_accessed=5*10**6,transcendentals=1024))(who,mine,other)


def cols(shape,axis): return lax.broadcasted_iota(jnp.int32,shape,axis)

def pair(a,b,ca):
    n=b.shape[1]
    h,l=split(b)
    both=dotg(a,jnp.concatenate([h,l],1),ca,0)
    return both[:,:n]+both[:,n:]

def early_kernel(trank,krank,tu,tv,om,top_ref):
    top=dotg(tv[...],om[...],0,0)
    live=(cols(top.shape,0)<trank[0])&(cols(top.shape,1)<krank[0])
    top_ref[...]=pair(tu[...],jnp.where(live,top,F32(0)),1)

def finish_kernel(who,m,rcat,ccat,tu,tv,om,top,row_ref,col_ref,nu_ref,nv_ref,rw,cw):
    ru=rcat.at[:,:256]; rv=rcat.at[:,256:]; cu=ccat.at[:,:256]; cv=ccat.at[:,256:]
    rr,cr,tr,kr=who[0],who[1],who[2],who[3]
    i=who[4]; j=who[5]
    for b in range(4):
        s=slice(256*b,256*b+256); e=256*b+256
        acc=dotg(m[s,:e],rv[:e,:],1,0)
        rw[s,:]=jnp.where(cols(acc.shape,1)<rr,acc,F32(0)).astype(BF)
        acc=dotg(m[s,:e],cv[:e,:],1,0)
        cw[s,:]=jnp.where(cols(acc.shape,1)<cr,acc,F32(0)).astype(BF)
    row_ref[...]=rw[pl.ds(pl.multiple_of(j*32,32),32),:]
    col_ref[...]=cw[pl.ds(pl.multiple_of(i*64,64),64),:]
    couple=dotg(rw[...],cw[...],0,0)
    low=dotg(cu[...],om[...],0,0)
    low=jnp.where(cols(low.shape,1)<kr,low,F32(0))
    mixed=dot3(couple,low,1,0)
    sample=top[...]-pair(ru[...],mixed,1)
    gram=dot3(sample,sample,0,0)
    eye=(cols(gram.shape,0)==cols(gram.shape,1))&(cols(gram.shape,0)>=kr)
    gram=gram+jnp.where(eye,F32(1),F32(0))
    _,W=factor([gram[8*g:8*g+8,:] for g in range(16)])
    W=jnp.concatenate(W,0)
    q=dot3(sample,W,1,1)
    nu_ref[...]=(q*F32(32)).astype(BF)
    ptop=pair(tu[...],q,0)
    ptop=jnp.where(cols(ptop.shape,0)<tr,ptop,F32(0))
    rproj=pair(ru[...],q,0)
    plow=dot3(couple,rproj,0,0)
    nv_ref[...]=(pair(tv[...],ptop,1)-pair(cu[...],plow,1)).astype(BF)

def early(trank,krank,tu,tv,om):
    return pl.pallas_call(early_kernel,out_shape=jax.ShapeDtypeStruct((1024,128),F32),
        in_specs=[pl.BlockSpec(memory_space=pltpu.SMEM)]*2+[pl.BlockSpec(memory_space=pltpu.VMEM)]*3,
        out_specs=pl.BlockSpec(memory_space=pltpu.VMEM),
        compiler_params=pltpu.CompilerParams(vmem_limit_bytes=16*2**20),name="early_sample")(trank,krank,tu,tv,om)

def finish(who,m,rcat,ccat,tu,tv,om,top):
    return pl.pallas_call(finish_kernel,
        out_shape=(jax.ShapeDtypeStruct((32,256),BF),jax.ShapeDtypeStruct((64,256),BF),
                   jax.ShapeDtypeStruct((1024,128),BF),jax.ShapeDtypeStruct((1024,128),BF)),
        in_specs=[pl.BlockSpec(memory_space=pltpu.SMEM)]+[pl.BlockSpec(memory_space=pltpu.VMEM)]*7,
        out_specs=(pl.BlockSpec(memory_space=pltpu.VMEM),)*4,
        scratch_shapes=[pltpu.VMEM((1024,256),BF)]*2,
        compiler_params=pltpu.CompilerParams(vmem_limit_bytes=24*2**20),name="recompress")(who,m,rcat,ccat,tu,tv,om,top)


def to_all(block):
    every=jnp.broadcast_to(block[None],(16,)+block.shape)
    return lax.all_to_all(every,"row",split_axis=0,concat_axis=0,tiled=True)


def per_device(diag_tile,row_u,row_v,col_u,col_v,tile_u,tile_v,omega,row_rank,col_rank,tile_rank,keep_rank):
    i=lax.axis_index("row").astype(jnp.int32); j=lax.axis_index("col").astype(jnp.int32)
    trank=tile_rank.reshape((1,)); krank=keep_rank.reshape((1,))
    tu=tile_u.reshape((1024,256)); tv=tile_v.reshape((1024,256))
    rcat=lax.all_gather(jnp.concatenate([row_u[0],row_v[0]],1),"col",axis=0,tiled=True)
    half=lax.dynamic_slice_in_dim(diag_tile,lax.bitwise_and(j,1)*32,32,0)
    mine=to_all(half)
    other=lax.ppermute(mine,"col",[(s,s^1) for s in range(32)])
    ccat=to_all(jnp.concatenate([col_u[0],col_v[0]],1)).reshape((1024,512))
    top=early(trank,krank,tu,tv,omega)
    strip,inverse=chol(jnp.stack([i,j]),mine,other)
    who=jnp.concatenate([row_rank,col_rank,trank,krank,i[None],j[None]])
    row_out,col_out,new_u,new_v=finish(who,inverse,rcat,ccat,tu,tv,omega,top)
    return (strip,row_out[None],col_out[None],new_u[None,None],new_v[None,None])


def solution(mesh):
    return jax.shard_map(
        per_device,
        mesh=mesh,
        in_specs=(P("row",None),P("row","col",None),P("row","col",None),P("col","row",None),P("col","row",None),
            P("row","col",None,None),P("row","col",None,None),P(),P("row"),P("col"),P("row","col"),P("row","col")),
        out_specs=(P("row",None),P("row","col",None),P("col","row",None),P("row","col",None,None),P("row","col",None,None)),
        check_vma=False)
```

time: 545 us -> 131 us (0.24)
  other arithmetic: 285 us -> 1.48 us
  blocking collectives: 121 us -> 22.4 us
  Pallas kernels: 0 us -> 65.8 us
  matrix products: 58.1 us -> 0 us
  local copies, waits for them, and re-layouts: 51.8 us -> 8.53 us
  starting transfers between devices: 0.04 us -> 8.79 us
  between operations: 22.8 us -> 16.7 us
  waiting for transfers between devices: 0.68 us -> 6.69 us
    another operation x38 -> x1, other arithmetic: 278 us -> 0.07 us  [per_device(): strip, inverse = chol(jnp.stack([i, j]), mine, other)]
    all_gather x4 -> x0, blocking collectives: 121 us -> none  [the longest x1 51.8 us: per_device(): lax.all_gather(rv, 'col', axis=1, tiled=True)]
    pallas_call x0 -> x3, Pallas kernels: none -> 65.8 us  [the longest x1 54.2 us: chol(): pl.pallas_call(chol_kernel, out_shape=(jax.ShapeDtypeStruct((64, 1024), F...]
    another operation x30 -> x0, matrix products: 46.5 us -> none  [the longest x14 23.1 us: per_device(): factor = jnp.linalg.cholesky(whole.astype(jnp.float32))]
    another operation x60 -> x0, local copies, waits for them, and re-layouts: 39.8 us -> none
    all_to_all x0 -> x1, blocking collectives: none -> 22.4 us  [to_all(): return lax.all_to_all(every, 'row', split_axis=0, concat_axis=0, tiled=True)]
    dot_general x14 -> x0, matrix products: 11.6 us -> none  [the longest x1 1.63 us: recompress(): jnp.dot(v_tile, proj_top, precision=HIGH)]
    all_gather x1, waiting for transfers between devices: 0.01 us -> 6.67 us  [per_device(): lax.all_gather(jnp.concatenate([row_u[0], row_v[0]], 1), 'col', axis=0, t...]
  transfers between devices with their start and end apart: 1 -> 3, of which waited for: 0 -> 1; matrix products, arithmetic and copies ran while one was open for 1% -> 2% of each run, Pallas kernels for 0% -> 42%
where the time goes in v1:
time: 131 us; the launch traced here: 130 us
  Pallas kernels  65.8 us (50%)
  blocking collectives  22.4 us (17%)
  between operations  16.7 us (13%)
  starting transfers between devices  8.79 us (7%)
  local copies, waits for them, and re-layouts  8.53 us (7%)
  waiting for transfers between devices  6.69 us (5%)
  other arithmetic  1.48 us (1%)
    pallas_call x1, Pallas kernels, chol(): pl.pallas_call(chol_kernel, out_shape=(jax.ShapeDtypeStruct((64, 1024), F...  54.2 us
    all_to_all x1, blocking collectives, to_all(): return lax.all_to_all(every, 'row', split_axis=0, concat_axis=0, tiled=True)  22.4 us
    pallas_call x1, Pallas kernels, finish(): pl.pallas_call(finish_kernel, out_shape=(jax.ShapeDtypeStruct((32, 256),...  11.1 us
    unnamed x26, local copies, waits for them, and re-layouts  7.23 us
    all_gather x1, waiting for transfers between devices, per_device(): lax.all_gather(jnp.concatenate([row_u[0], row_v[0]], 1), 'col', axis=0, t...  6.67 us
    ppermute x1, starting transfers between devices, per_device(): other = lax.ppermute(mine, 'col', [(s, s ^ 1) for s in range(32)])  5.1 us
    all_to_all x1, starting transfers between devices, to_all(): return lax.all_to_all(every, 'row', split_axis=0, concat_axis=0, tiled=True)  3.65 us
  transfers between devices with their start and end apart: 3, of which 1 were waited for; matrix products, arithmetic and copies ran while one was open for 2% of the time, Pallas kernels for 42%

profile of v1, /device:TPU:1, one launch (start us, length us, event | category | flops | bytes accessed | tf_op | source)
XLA Modules:
  0.0 130.5 jit_solution(5270302956524434267)
XLA Ops:
  7.2 0.0 copy-start
  7.2 0.0 copy-start.11
  7.2 0.0 all-gather.2.cloned.1.call-start
  7.2 0.8 copy-done
  8.1 0.0 copy-start.12
  8.1 0.1 broadcast_in_dim.12
  8.2 22.4 %all_to_all.10.mine = bf16[16,32,1024]{2,1,0:T(8,128)(2,1)S(1)} all-to-all(bf16[16,32,1024]{2,1,0:T(8,128)(2,1)S(1)} %broadcast_in_dim.12), channel_id=1, replica_groups=mesh['row'=16,'col'=32] {'row'}, dimensions={0} | all-to-all | bytes 2097152 | tf_op jit(solution)/shard_map/all_to_all | solution.py:171
  30.6 0.0 copy-start.8
  30.6 0.0 copy-start.1
  30.6 0.0 copy-start.3
  30.6 0.0 copy-start.7
  30.6 5.1 %collective-permute-start = (bf16[16,32,1024]{2,1,0:T(8,128)(2,1)S(1)}, bf16[16,32,1024]{2,1,0:T(8,128)(2,1)}, u32[]{:S(2)}, u32[]{:S(2)}) collective-permute-start(bf16[16,32,1024]{2,1,0:T(8,128)(2,1)S(1)} %all_to_all.10.mine), channel_id=1, source_target_pairs={{0,1},{1,0},{2,3},{3,2},{4,5},{5,4},{6,7},{7,6},{8,9},{9,8},{10,11... | collective-permute-start | bytes 3145736 | tf_op jit(solution)/shard_map/ppermute | solution.py:181
  35.7 0.0 copy-done.11
  35.7 0.0 copy-done.12
  35.7 0.6 pad_maximum_fusion.1
  36.4 0.0 all-gather.2.cloned.1.call-update
  36.4 0.8 pad_maximum_fusion
  37.2 1.1 broadcast_in_dim.13
  38.3 3.7 %all-to-all-start.1 = ((bf16[16,64,512]{2,1,0:T(8,128)(2,1)}), bf16[16,64,512]{2,1,0:T(8,128)(2,1)S(1)}, u32[]{:S(2)}, u32[]{:S(2)}) async-start(bf16[16,64,512]{2,1,0:T(8,128)(2,1)} %broadcast_in_dim.13), calls=%async_computation.1 | async-start | bytes 2097152 | tf_op jit(solution)/shard_map/all_to_all | solution.py:171
  44.5 0.0 copy-done.1
  44.5 0.0 copy-done.3
  44.5 0.0 copy-done.7
  44.5 0.6 early_sample.1.top
  45.2 0.0 copy-done.8
  45.2 0.0 copy-start.5
  45.2 0.8 copy-done.5
  46.0 0.1 concatenate.9.who
  46.1 0.1 pad_add_fusion.who
  46.1 0.0 collective-permute-done.other
  46.1 0.0 copy-start.9
  46.1 1.2 copy-done.9
  47.4 54.2 %chol_inverse.1 = (f32[64,1024]{1,0:T(8,128)}, bf16[1024,1024]{1,0:T(8,128)(2,1)S(1)}) custom-call(s32[2]{0:T(128)S(1)} %pad_add_fusion.who, bf16[16,32,1024]{2,1,0:T(8,128)(2,1)S(1)} %copy-done.9, bf16[16,32,1024]{2,1,0:T(8,128)(2,1)} %collective-permute-done.other), custom_call_target="tpu_custom_call" | custom-call | flops 30000001024 | bytes 5000000 | tf_op jit(solution)/shard_map/chol_inverse/pallas_call | solution.py:101
  101.5 0.0 all-to-all-done.1
  101.5 6.7 %all-gather.2.cloned.1.call-done.rcat = bf16[1024,512]{1,0:T(8,128)(2,1)} async-done(((bf16[32,512]{1,0:T(8,128)(2,1)}), bf16[1024,512]{1,0:T(8,128)(2,1)}) %all-gather.2.cloned.1.call-update) | async-done | bytes 1048592 | tf_op jit(solution)/shard_map/all_gather | solution.py:178
  108.2 0.0 copy-start.2
  108.2 1.0 copy-done.2
  109.2 0.0 copy-start.4
  109.2 1.0 copy-done.4
  110.3 0.0 copy-start.6
  110.3 1.0 copy-done.6
  111.3 0.0 copy-start.10
  111.3 1.2 copy-done.10
  112.6 11.1 %recompress.1 = (bf16[32,256]{1,0:T(8,128)(2,1)}, bf16[64,256]{1,0:T(8,128)(2,1)}, bf16[1024,128]{1,0:T(8,128)(2,1)}, bf16[1024,128]{1,0:T(8,128)(2,1)}) custom-call(s32[6]{0:T(128)S(1)} %concatenate.9.who, bf16[1024,1024]{1,0:T(8,128)(2,1)S(1)} %get-tuple-element.12.m, bf16[1024,512]{1,0:T(8,128)(2,1)S(1)} %copy-done.10, bf16[1024,512]{1,0:T(8,128)(2,1)S(1)} %bitcast.19, ...), custom_call_target="tpu_custom_call" | custom-call | tf_op jit(solution)/shard_map/recompress/pallas_call | solution.py:160
  (1 shorter events, 0.0 us)
Async XLA Ops:
  7.2 0.9 copy-start
  7.2 28.5 %copy-start.11 = (bf16[1,32,256]{2,1,0:T(8,128)(2,1)S(1)}, bf16[1,32,256]{2,1,0:T(8,128)(2,1)}, u32[]{:S(2)}) copy-start(bf16[1,32,256]{2,1,0:T(8,128)(2,1)} %param.14) | copy-start | bytes 49156
  7.2 101.0 %all-gather.2.cloned.1.call-start = ((), (), s32[]{:S(2)}) async-start(), calls=%async_computation.2 | async-start | bytes 1081344 | tf_op jit(solution)/shard_map/all_gather | solution.py:178
  8.1 27.7 %copy-start.12 = (bf16[1,32,256]{2,1,0:T(8,128)(2,1)S(1)}, bf16[1,32,256]{2,1,0:T(8,128)(2,1)}, u32[]{:S(2)}) copy-start(bf16[1,32,256]{2,1,0:T(8,128)(2,1)} %param.13) | copy-start | bytes 49156
  30.6 14.6 %copy-start.8 = (bf16[16,32,1024]{2,1,0:T(8,128)(2,1)}, bf16[16,32,1024]{2,1,0:T(8,128)(2,1)S(1)}, u32[]{:S(2)}) copy-start(bf16[16,32,1024]{2,1,0:T(8,128)(2,1)S(1)} %all_to_all.10.mine) | copy-start | bytes 3145732
  30.6 13.9 %copy-start.1 = (bf16[1,1,1024,256]{3,2,1,0:T(8,128)(2,1)S(1)}, bf16[1,1,1024,256]{3,2,1,0:T(8,128)(2,1)}, u32[]{:S(2)}) copy-start(bf16[1,1,1024,256]{3,2,1,0:T(8,128)(2,1)} %param.17) | copy-start | bytes 1572868
  30.6 13.9 %copy-start.3 = (bf16[1,1,1024,256]{3,2,1,0:T(8,128)(2,1)S(1)}, bf16[1,1,1024,256]{3,2,1,0:T(8,128)(2,1)}, u32[]{:S(2)}) copy-start(bf16[1,1,1024,256]{3,2,1,0:T(8,128)(2,1)} %param.18) | copy-start | bytes 1572868
  30.6 13.9 %copy-start.7 = (bf16[1024,128]{1,0:T(8,128)(2,1)S(1)}, bf16[1024,128]{1,0:T(8,128)(2,1)}, u32[]{:S(2)}) copy-start(bf16[1024,128]{1,0:T(8,128)(2,1)} %om.3) | copy-start | bytes 786436
  30.6 15.5 %collective-permute-start = (bf16[16,32,1024]{2,1,0:T(8,128)(2,1)S(1)}, bf16[16,32,1024]{2,1,0:T(8,128)(2,1)}, u32[]{:S(2)}, u32[]{:S(2)}) collective-permute-start(bf16[16,32,1024]{2,1,0:T(8,128)(2,1)S(1)} %all_to_all.10.mine), channel_id=1, source_target_pairs={{0,1},{1,0},{2,3},{3,2},{4,5},{5,4},{6,7},{7,6},{8,9},{9,8},{10,11... | collective-permute-start | bytes 3145736 | tf_op jit(solution)/shard_map/ppermute | solution.py:181
  38.3 63.3 %all-to-all-start.1 = ((bf16[16,64,512]{2,1,0:T(8,128)(2,1)}), bf16[16,64,512]{2,1,0:T(8,128)(2,1)S(1)}, u32[]{:S(2)}, u32[]{:S(2)}) async-start(bf16[16,64,512]{2,1,0:T(8,128)(2,1)} %broadcast_in_dim.13), calls=%async_computation.1 | async-start | bytes 2097152 | tf_op jit(solution)/shard_map/all_to_all | solution.py:171
  45.2 0.8 copy-start.5
  46.1 1.2 copy-start.9
  108.2 1.0 copy-start.2
  109.2 1.0 copy-start.4
  110.3 1.0 copy-start.6
  111.3 1.2 copy-start.10
Sparse Core Ops, SparseCore 0:
  36.5 71.6 all-gather.1

commit v2 on v1

v2 whole, which is shorter than its diff:
```python
import jax, jax.numpy as jnp
from jax import lax
from jax.sharding import PartitionSpec as P
from jax.experimental import pallas as pl
from jax.experimental.pallas import tpu as pltpu
F32=jnp.float32; BF=jnp.bfloat16
G=8

def lane(x,c): return jnp.broadcast_to(x[:,c:c+1],(8,128))
def sub(x,s): return jnp.broadcast_to(x[s:s+1,:],(8,128))

AHEAD=2


def factor(S):
    row=lax.broadcasted_iota(jnp.int32,(8,128),0); col=lax.broadcasted_iota(jnp.int32,(8,128),1)
    W=[jnp.where(col==row+8*g,F32(1),F32(0)) for g in range(16)]
    S=list(S)
    late=None
    ahead=None
    for p in range(16):
        C=[lane(S[p],8*p+j) for j in range(8)] if ahead is None else ahead
        if late is not None:
            for g in range(p+AHEAD,16):
                S[g]=S[g]-late[8*g:8*g+8,:128]; W[g]=W[g]-late[8*g:8*g+8,128:]
        near=range(p+1,min(p+1+AHEAD+(1-p%2),16))
        T={g:[lane(S[g],8*p+j) for j in range(8)] for g in near}
        ahead=[lane(S[p+1],8*p+8+j) for j in range(8)] if p<15 else None
        a=[[sub(C[j],i) if i>=j else None for j in range(8)] for i in range(8)]
        B=[sub(S[p],j) for j in range(8)]; V=[sub(W[p],j) for j in range(8)]
        for j in range(8):
            r=lax.rsqrt(a[j][j])
            l=[None]*8
            for i in range(j+1,8): l[i]=a[i][j]*r
            for i in range(j+1,8):
                for k in range(j+1,i+1): a[i][k]=a[i][k]-l[i]*l[k]
            for X in [B,V]+list(T.values()):
                X[j]=X[j]*r
                for i in range(j+1,8): X[i]=X[i]-l[i]*X[j]
        if p<15:
            N=T[p+1]
            for k in range(8):
                for j in range(8): ahead[k]=ahead[k]-N[j]*sub(N[j],k)
        S[p]=B[0]; W[p]=V[0]
        for j in range(1,8):
            S[p]=jnp.where(row==j,B[j],S[p]); W[p]=jnp.where(row==j,V[j],W[p])
        for g in near:
            t=[T[g][j]*B[j] for j in range(8)]; u=[T[g][j]*V[j] for j in range(8)]
            S[g]=S[g]-(((t[0]+t[1])+(t[2]+t[3]))+((t[4]+t[5])+(t[6]+t[7])))
            W[g]=W[g]-(((u[0]+u[1])+(u[2]+u[3]))+((u[4]+u[5])+(u[6]+u[7])))
        late=None
        if p%2 and p+1+AHEAD<16:
            both=[jnp.concatenate([S[g],W[g]],1) for g in (p-1,p)]
            high=[x.astype(BF).astype(F32) for x in both]
            low=[x-h for x,h in zip(both,high)]
            left=[x[:,:128] for x in high]
            lhs=jnp.concatenate(left+[x[:,:128] for x in low]+left,0).astype(BF)
            rhs=jnp.concatenate(high+high+low,0).astype(BF)
            late=dotg(lhs,rhs,0,0)
    return S,W


def split(x):
    h=x.astype(BF); return h,(x-h.astype(F32)).astype(BF)
def dotg(a,b,ca,cb): return lax.dot_general(a,b,(((ca,),(cb,)),((),())),preferred_element_type=F32)
def dot3(a,b,ca,cb):
    ah,al=split(a); bh,bl=split(b)
    return dotg(ah,bh,ca,cb)+(dotg(ah,bl,ca,cb)+dotg(al,bh,ca,cb))

def chol_kernel(mine_any,other_any,l_ref,m_ref,buf,lout,mine,other,sems):
    N=1024; nb=8
    strip=lax.axis_index("row").astype(jnp.int32)
    c=lax.bitwise_and(lax.axis_index("col").astype(jnp.int32),1)*32
    copies=[pltpu.make_async_copy(mine_any,mine,sems.at[0]),pltpu.make_async_copy(other_any,other,sems.at[1])]
    for x in copies: x.start()
    for x in copies: x.wait()
    for s in range(16):
        w=128*(s//2+1)
        buf[pl.ds(pl.multiple_of(64*s+c,32),32),:w]=mine[s,:,:w].astype(F32)
        buf[pl.ds(pl.multiple_of(64*s+32-c,32),32),:w]=other[s,:,:w].astype(F32)
    row=lax.broadcasted_iota(jnp.int32,(8,128),0); col=lax.broadcasted_iota(jnp.int32,(8,128),1)
    D=buf[:128,:128]
    for k in range(nb):
        k0=128*k; n0=k0+128
        S,W=factor([D[8*g:8*g+8,:] for g in range(16)])
        M=jnp.concatenate(W,0)
        mh,ml=split(M)
        m_ref[k0:n0,k0:n0]=mh
        R=jnp.concatenate([jnp.where(col>=row+8*g,S[g],F32(0)) for g in range(16)],0)
        lout[k0:n0,k0:n0]=R.T
        if k:
            ph,plo=split(buf[k0:n0,:k0])
            pan=dotg(mh,ph,1,0)+(dotg(mh,plo,1,0)+dotg(ml,ph,1,0))
            m_ref[k0:n0,:k0]=pan.astype(BF)
        if k==nb-1: break
        lout[k0:n0,n0:]=jnp.zeros((128,N-n0),F32)
        m_ref[k0:n0,n0:]=jnp.zeros((128,N-n0),BF)
        lh,ll=split(buf[n0:,k0:n0])
        lc=dotg(lh,mh,1,1)+(dotg(lh,ml,1,1)+dotg(ll,mh,1,1))
        lout[n0:,k0:n0]=lc
        ch,cl=split(lc)
        lhs=jnp.concatenate([ch,cl,ch],1); rhs=jnp.concatenate([ch,ch,cl],1)
        D=buf[n0:n0+128,n0:n0+128]-dotg(lhs[:128],rhs[:128],1,1)
        qh,ql=(mh,ml) if k==0 else split(jnp.concatenate([pan,M],1))
        inv=jnp.concatenate([qh,qh,ql],0)
        up=dotg(lhs,inv,1,0)
        if k: buf[n0:,:k0]=buf[n0:,:k0]-up[:,:k0]
        buf[n0:,k0:n0]=-up[:,k0:]
        for c0 in range(n0+128,N,256):
            c1=min(c0+256,N)
            buf[c0:c1,n0:c1]=buf[c0:c1,n0:c1]-dotg(lhs[c0-n0:c1-n0],rhs[:c1-n0],1,1)
    l_ref[...]=lout[pl.ds(pl.multiple_of(strip*64,64),64),:]

def chol(mine,other):
    return pl.pallas_call(chol_kernel,
        out_shape=(jax.ShapeDtypeStruct((64,1024),F32),jax.ShapeDtypeStruct((1024,1024),BF)),
        in_specs=[pl.BlockSpec(memory_space=pl.ANY)]*2,
        out_specs=(pl.BlockSpec(memory_space=pltpu.VMEM),)*2,
        scratch_shapes=[pltpu.VMEM((1024,1024),F32)]*2+[pltpu.VMEM((16,32,1024),BF)]*2+[pltpu.SemaphoreType.DMA((2,))],
        compiler_params=pltpu.CompilerParams(vmem_limit_bytes=58*2**20),
        name="chol_inverse",cost_estimate=pl.CostEstimate(flops=10**9,bytes_accessed=10**6,transcendentals=1024))(mine,other)


def cols(shape,axis): return lax.broadcasted_iota(jnp.int32,shape,axis)

def pair(a,b,ca):
    n=b.shape[1]
    h,l=split(b)
    both=dotg(a,jnp.concatenate([h,l],1),ca,0)
    return both[:,:n]+both[:,n:]

def finish_kernel(rrank,crank,trank,krank,m_any,rcat_any,ccat_any,tu_any,tv_any,om_any,row_ref,col_ref,nu_ref,nv_ref,
                  rw,cw,rcat,tu,tv,om,m,ccat,sems):
    moves=[pltpu.make_async_copy(x,y,sems.at[n]) for n,(x,y) in enumerate(((ccat_any,ccat),(m_any,m),(rcat_any,rcat),(om_any,om),(tv_any,tv),(tu_any,tu)))]
    for x in moves: x.start()
    rr,cr,tr,kr=rrank[0],crank[0],trank[0,0],krank[0,0]
    i=lax.axis_index("row").astype(jnp.int32); j=lax.axis_index("col").astype(jnp.int32)
    ru=rcat.at[:,:256]; rv=rcat.at[:,256:]; cu=ccat.at[:,:256]; cv=ccat.at[:,256:]
    for x in moves[:2]: x.wait()
    for b in range(4):
        s=slice(256*b,256*b+256); e=256*b+256
        acc=dotg(m[s,:e],cv[:e,:],1,0)
        cw[s,:]=jnp.where(cols(acc.shape,1)<cr,acc,F32(0)).astype(BF)
    for x in moves[2:]: x.wait()
    for b in range(4):
        s=slice(256*b,256*b+256); e=256*b+256
        acc=dotg(m[s,:e],rv[:e,:],1,0)
        rw[s,:]=jnp.where(cols(acc.shape,1)<rr,acc,F32(0)).astype(BF)
    row_ref[...]=rw[pl.ds(pl.multiple_of(j*32,32),32),:]
    col_ref[...]=cw[pl.ds(pl.multiple_of(i*64,64),64),:]
    inner=dotg(tv[...],om[...],0,0)
    inner=jnp.where((cols(inner.shape,0)<tr)&(cols(inner.shape,1)<kr),inner,F32(0))
    top=pair(tu[...],inner,1)
    couple=dotg(rw[...],cw[...],0,0)
    low=dotg(cu[...],om[...],0,0)
    low=jnp.where(cols(low.shape,1)<kr,low,F32(0))
    mixed=dot3(couple,low,1,0)
    sample=top-pair(ru[...],mixed,1)
    gram=dot3(sample,sample,0,0)
    eye=(cols(gram.shape,0)==cols(gram.shape,1))&(cols(gram.shape,0)>=kr)
    gram=gram+jnp.where(eye,F32(1),F32(0))
    _,W=factor([gram[8*g:8*g+8,:] for g in range(16)])
    W=jnp.concatenate(W,0)
    q=dot3(sample,W,1,1)
    nu_ref[...]=(q*F32(32)).astype(BF)
    ptop=pair(tu[...],q,0)
    ptop=jnp.where(cols(ptop.shape,0)<tr,ptop,F32(0))
    rproj=pair(ru[...],q,0)
    plow=dot3(couple,rproj,0,0)
    nv_ref[...]=(pair(tv[...],ptop,1)-pair(cu[...],plow,1)).astype(BF)

def finish(rrank,crank,trank,krank,m,rcat,ccat,tu,tv,om):
    smem=pl.BlockSpec(memory_space=pltpu.SMEM); vmem=pl.BlockSpec(memory_space=pltpu.VMEM); far=pl.BlockSpec(memory_space=pl.ANY)
    return pl.pallas_call(finish_kernel,
        out_shape=(jax.ShapeDtypeStruct((32,256),BF),jax.ShapeDtypeStruct((64,256),BF),
                   jax.ShapeDtypeStruct((1024,128),BF),jax.ShapeDtypeStruct((1024,128),BF)),
        in_specs=[smem]*4+[far]*6,
        out_specs=(vmem,)*4,
        scratch_shapes=[pltpu.VMEM((1024,256),BF)]*2+[pltpu.VMEM((1024,512),BF)]+[pltpu.VMEM((1024,256),BF)]*2
            +[pltpu.VMEM((1024,128),BF),pltpu.VMEM((1024,1024),BF),pltpu.VMEM((1024,512),BF),pltpu.SemaphoreType.DMA((6,))],
        compiler_params=pltpu.CompilerParams(vmem_limit_bytes=58*2**20),name="recompress")(rrank,crank,trank,krank,m,rcat,ccat,tu,tv,om)


def to_all(block):
    every=jnp.broadcast_to(block[None],(16,)+block.shape)
    return lax.all_to_all(every,"row",split_axis=0,concat_axis=0,tiled=True)


def per_device(diag_tile,row_u,row_v,col_u,col_v,tile_u,tile_v,omega,row_rank,col_rank,tile_rank,keep_rank):
    core=lax.bitwise_and(lax.axis_index("col").astype(jnp.int32),1)
    rows=jnp.concatenate([row_u[0],row_v[0]],1)
    half=lax.dynamic_slice_in_dim(diag_tile,core*32,32,0)
    half,rows=lax.optimization_barrier((half,rows))
    rcat=lax.all_gather(rows,"col",axis=0,tiled=True)
    mine=to_all(half)
    other=lax.ppermute(mine,"col",[(s,s^1) for s in range(32)])
    ccat=to_all(jnp.concatenate([col_u[0],col_v[0]],1)).reshape((1024,512))
    strip,inverse=chol(mine,other)
    row_out,col_out,new_u,new_v=finish(row_rank,col_rank,tile_rank,keep_rank,inverse,rcat,ccat,
        tile_u.reshape((1024,256)),tile_v.reshape((1024,256)),omega)
    return (strip,row_out[None],col_out[None],new_u[None,None],new_v[None,None])


def solution(mesh):
    return jax.shard_map(
        per_device,
        mesh=mesh,
        in_specs=(P("row",None),P("row","col",None),P("row","col",None),P("col","row",None),P("col","row",None),
            P("row","col",None,None),P("row","col",None,None),P(),P("row"),P("col"),P("row","col"),P("row","col")),
        out_specs=(P("row",None),P("row","col",None),P("col","row",None),P("row","col",None,None),P("row","col",None,None)),
        check_vma=False)
```

time: 131 us -> 115 us (0.88)
  waiting for transfers between devices: 6.69 us -> 36 us
  Pallas kernels: 65.8 us -> 39.5 us
  blocking collectives: 22.4 us -> 0 us
  starting transfers between devices: 8.79 us -> 17 us
  local copies, waits for them, and re-layouts: 8.53 us -> 4.11 us
    pallas_call x1, Pallas kernels: 54.2 us -> 29.4 us  [chol(): pl.pallas_call(chol_kernel, out_shape=(jax.ShapeDtypeStruct((64, 1024), F...]
    all_to_all x1 -> x0, blocking collectives: 22.4 us -> none  [to_all(): return lax.all_to_all(every, 'row', split_axis=0, concat_axis=0, tiled=True)]
    all_gather x1, waiting for transfers between devices: 6.67 us -> 21.8 us  [per_device(): rcat = lax.all_gather(rows, 'col', axis=0, tiled=True)]
    all_to_all x1 -> x2, waiting for transfers between devices: 0.01 us -> 13.5 us  [to_all(): return lax.all_to_all(every, 'row', split_axis=0, concat_axis=0, tiled=True)]
    all_to_all x1 -> x2, starting transfers between devices: 3.65 us -> 11.2 us  [to_all(): return lax.all_to_all(every, 'row', split_axis=0, concat_axis=0, tiled=True)]
    unnamed x26 -> x12, local copies, waits for them, and re-layouts: 7.23 us -> 1.89 us
  transfers between devices with their start and end apart: 3 -> 4, of which waited for: 1 -> 2; matrix products, arithmetic and copies ran while one was open for 2% -> 1% of each run, Pallas kernels for 42% -> 26%
where the time goes in v2:
time: 115 us
  Pallas kernels  39.5 us (34%)
  waiting for transfers between devices  36 us (31%)
  starting transfers between devices  17 us (15%)
  between operations  16.8 us (15%)
  local copies, waits for them, and re-layouts  4.11 us (4%)
  other arithmetic  1.36 us (1%)
    pallas_call x1, Pallas kernels, chol(): pl.pallas_call(chol_kernel, out_shape=(jax.ShapeDtypeStruct((64, 1024), F...  29.4 us
    all_gather x1, waiting for transfers between devices, per_device(): rcat = lax.all_gather(rows, 'col', axis=0, tiled=True)  21.8 us
    all_to_all x2, waiting for transfers between devices, to_all(): return lax.all_to_all(every, 'row', split_axis=0, concat_axis=0, tiled=True)  13.5 us
    all_to_all x2, starting transfers between devices, to_all(): return lax.all_to_all(every, 'row', split_axis=0, concat_axis=0, tiled=True)  11.2 us
    pallas_call x1, Pallas kernels, finish(): pl.pallas_call(finish_kernel, out_shape=(jax.ShapeDtypeStruct((32, 256),...  10.2 us
    ppermute x1, starting transfers between devices, per_device(): other = lax.ppermute(mine, 'col', [(s, s ^ 1) for s in range(32)])  5.73 us
  transfers between devices with their start and end apart: 4, of which 2 were waited for; matrix products, arithmetic and copies ran while one was open for 1% of the time, Pallas kernels for 26%

profile of v2, /device:TPU:1, one launch (start us, length us, event | category | flops | bytes accessed | tf_op | source)
XLA Modules:
  0.0 114.7 jit_solution(14378206200274835312)
XLA Ops:
  7.2 0.0 copy-start
  7.2 0.0 copy-start.4
  7.2 0.0 copy-start.3
  7.2 0.9 copy-done
  8.1 1.4 %pad_maximum_fusion.1 = bf16[32,512]{1,0:T(8,128)(2,1)} fusion(bf16[32,256]{1,0:T(8,128)(2,1)} %bitcast.16, bf16[32,256]{1,0:T(8,128)(2,1)} %bitcast.17), kind=kLoop, calls=%fused_computation.1 | loop fusion | flops 65536 | bytes 65536 | tf_op jit(solution)/shard_map/concatenate | solution.py:191
  9.4 1.1 broadcast_in_dim.24
  10.5 7.6 %all-to-all-start = ((bf16[16,32,1024]{2,1,0:T(8,128)(2,1)}), bf16[16,32,1024]{2,1,0:T(8,128)(2,1)S(1)}, u32[]{:S(2)}, u32[]{:S(2)}) async-start(bf16[16,32,1024]{2,1,0:T(8,128)(2,1)} %broadcast_in_dim.24), calls=%async_computation | async-start | bytes 2097152 | tf_op jit(solution)/shard_map/all_to_all | solution.py:186
  18.1 0.0 all-gather.2.cloned.1.call-start
  18.2 0.7 all-gather.2.cloned.1.call-update
  18.9 13.5 %all-to-all-done.mine_any = bf16[16,32,1024]{2,1,0:T(8,128)(2,1)S(1)} async-done(((bf16[16,32,1024]{2,1,0:T(8,128)(2,1)}), bf16[16,32,1024]{2,1,0:T(8,128)(2,1)S(1)}, u32[]{:S(2)}, u32[]{:S(2)}) %all-to-all-start) | async-done | bytes 1048608 | tf_op jit(solution)/shard_map/all_to_all | solution.py:186
  32.4 0.0 copy-start.2
  32.4 5.7 %collective-permute-start = (bf16[16,32,1024]{2,1,0:T(8,128)(2,1)S(1)}, bf16[16,32,1024]{2,1,0:T(8,128)(2,1)S(1)}, u32[]{:S(2)}, u32[]{:S(2)}) collective-permute-start(bf16[16,32,1024]{2,1,0:T(8,128)(2,1)S(1)} %all-to-all-done.mine_any), channel_id=1, source_target_pairs={{0,1},{1,0},{2,3},{3,2},{4,5},{5,4},{6,7},{7,6},{8,9},{9,8},{10,11... | collective-permute-start | bytes 3145736 | tf_op jit(solution)/shard_map/ppermute | solution.py:196
  38.1 0.0 copy-done.4
  38.1 0.0 copy-done.3
  38.1 1.1 broadcast_in_dim.25
  39.2 3.7 %all-to-all-start.1 = ((bf16[16,64,512]{2,1,0:T(8,128)(2,1)}), bf16[16,64,512]{2,1,0:T(8,128)(2,1)S(1)}, u32[]{:S(2)}, u32[]{:S(2)}) async-start(bf16[16,64,512]{2,1,0:T(8,128)(2,1)} %broadcast_in_dim.25), calls=%async_computation.1 | async-start | bytes 2097152 | tf_op jit(solution)/shard_map/all_to_all | solution.py:186
  45.5 0.0 collective-permute-done.other_any
  45.5 0.0 copy-done.2
  45.5 0.0 copy-start.5
  45.5 1.0 copy-done.5
  46.5 29.4 %chol_inverse.1 = (f32[64,1024]{1,0:T(8,128)}, bf16[1024,1024]{1,0:T(8,128)(2,1)}) custom-call(bf16[16,32,1024]{2,1,0:T(8,128)(2,1)} %copy-done.2, bf16[16,32,1024]{2,1,0:T(8,128)(2,1)} %copy-done.5), custom_call_target="tpu_custom_call" | custom-call | flops 1000000000 | bytes 1000000 | tf_op jit(solution)/shard_map/chol_inverse/pallas_call | solution.py:115
  75.9 0.0 all-to-all-done.1
  75.9 0.0 copy-start.1
  75.9 21.8 %all-gather.2.cloned.1.call-done.rcat_any = bf16[1024,512]{1,0:T(8,128)(2,1)} async-done(((bf16[32,512]{1,0:T(8,128)(2,1)}), bf16[1024,512]{1,0:T(8,128)(2,1)}) %all-gather.2.cloned.1.call-update) | async-done | bytes 1048592 | tf_op jit(solution)/shard_map/all_gather | solution.py:194
  97.7 0.0 copy-done.1
  97.7 10.2 %recompress.1 = (bf16[32,256]{1,0:T(8,128)(2,1)}, bf16[64,256]{1,0:T(8,128)(2,1)}, bf16[1024,128]{1,0:T(8,128)(2,1)}, bf16[1024,128]{1,0:T(8,128)(2,1)}) custom-call(s32[1]{0:T(128)S(6)} %copy.17.rrank, s32[1]{0:T(128)S(6)} %copy.18.crank, s32[1,1]{1,0:T(1,128)S(6)} %copy.19.trank, s32[1,1]{1,0:T(1,128)S(6)} %copy.20.krank, ...), custom_call_target="tpu_custom_call" | custom-call | tf_op jit(solution)/shard_map/recompress/pallas_call | solution.py:174
  (2 shorter events, 0.0 us)
Async XLA Ops:
  7.2 0.9 copy-start
  7.2 30.9 %copy-start.4 = (bf16[1,64,256]{2,1,0:T(8,128)(2,1)S(1)}, bf16[1,64,256]{2,1,0:T(8,128)(2,1)}, u32[]{:S(2)}) copy-start(bf16[1,64,256]{2,1,0:T(8,128)(2,1)} %param.15) | copy-start | bytes 98308
  7.2 30.9 %copy-start.3 = (bf16[1,64,256]{2,1,0:T(8,128)(2,1)S(1)}, bf16[1,64,256]{2,1,0:T(8,128)(2,1)}, u32[]{:S(2)}) copy-start(bf16[1,64,256]{2,1,0:T(8,128)(2,1)} %param.16) | copy-start | bytes 98308
  10.5 21.8 %all-to-all-start = ((bf16[16,32,1024]{2,1,0:T(8,128)(2,1)}), bf16[16,32,1024]{2,1,0:T(8,128)(2,1)S(1)}, u32[]{:S(2)}, u32[]{:S(2)}) async-start(bf16[16,32,1024]{2,1,0:T(8,128)(2,1)} %broadcast_in_dim.24), calls=%async_computation | async-start | bytes 2097152 | tf_op jit(solution)/shard_map/all_to_all | solution.py:186
  18.1 79.6 %all-gather.2.cloned.1.call-start = ((), (), s32[]{:S(2)}) async-start(), calls=%async_computation.2 | async-start | bytes 1081344 | tf_op jit(solution)/shard_map/all_gather | solution.py:194
  32.4 13.1 %copy-start.2 = (bf16[16,32,1024]{2,1,0:T(8,128)(2,1)}, bf16[16,32,1024]{2,1,0:T(8,128)(2,1)S(1)}, u32[]{:S(2)}) copy-start(bf16[16,32,1024]{2,1,0:T(8,128)(2,1)S(1)} %all-to-all-done.mine_any) | copy-start | bytes 3145732
  32.4 13.1 %collective-permute-start = (bf16[16,32,1024]{2,1,0:T(8,128)(2,1)S(1)}, bf16[16,32,1024]{2,1,0:T(8,128)(2,1)S(1)}, u32[]{:S(2)}, u32[]{:S(2)}) collective-permute-start(bf16[16,32,1024]{2,1,0:T(8,128)(2,1)S(1)} %all-to-all-done.mine_any), channel_id=1, source_target_pairs={{0,1},{1,0},{2,3},{3,2},{4,5},{5,4},{6,7},{7,6},{8,9},{9,8},{10,11... | collective-permute-start | bytes 3145736 | tf_op jit(solution)/shard_map/ppermute | solution.py:196
  39.2 36.6 %all-to-all-start.1 = ((bf16[16,64,512]{2,1,0:T(8,128)(2,1)}), bf16[16,64,512]{2,1,0:T(8,128)(2,1)S(1)}, u32[]{:S(2)}, u32[]{:S(2)}) async-start(bf16[16,64,512]{2,1,0:T(8,128)(2,1)} %broadcast_in_dim.25), calls=%async_computation.1 | async-start | bytes 2097152 | tf_op jit(solution)/shard_map/all_to_all | solution.py:186
  45.5 1.0 copy-start.5
  75.9 21.8 %copy-start.1 = (bf16[16,64,512]{2,1,0:T(8,128)(2,1)}, bf16[16,64,512]{2,1,0:T(8,128)(2,1)S(1)}, u32[]{:S(2)}) copy-start(bf16[16,64,512]{2,1,0:T(8,128)(2,1)S(1)} %all-to-all-done.1) | copy-start | bytes 3145732
Sparse Core Ops, SparseCore 0:
  21.7 75.9 all-gather.1

commit v3 on v2

--- a/solution.py
+++ b/solution.py
@@ -118,7 +118,7 @@
         out_specs=(pl.BlockSpec(memory_space=pltpu.VMEM),)*2,
         scratch_shapes=[pltpu.VMEM((1024,1024),F32)]*2+[pltpu.VMEM((16,32,1024),BF)]*2+[pltpu.SemaphoreType.DMA((2,))],
         compiler_params=pltpu.CompilerParams(vmem_limit_bytes=58*2**20),
-        name="chol_inverse",cost_estimate=pl.CostEstimate(flops=10**9,bytes_accessed=10**6,transcendentals=1024))(mine,other)
+        name="chol_inverse",cost_estimate=pl.CostEstimate(flops=3*10**10,bytes_accessed=5*10**6,transcendentals=1024))(mine,other)
 
 
 def cols(shape,axis): return lax.broadcasted_iota(jnp.int32,shape,axis)
@@ -129,19 +129,27 @@
     both=dotg(a,jnp.concatenate([h,l],1),ca,0)
     return both[:,:n]+both[:,n:]
 
-def finish_kernel(rrank,crank,trank,krank,m_any,rcat_any,ccat_any,tu_any,tv_any,om_any,row_ref,col_ref,nu_ref,nv_ref,
+def finish_kernel(rrank,crank,trank,krank,m_any,rmine,rother,cblocks,tu_any,tv_any,om_any,row_ref,col_ref,nu_ref,nv_ref,
                   rw,cw,rcat,tu,tv,om,m,ccat,sems):
-    moves=[pltpu.make_async_copy(x,y,sems.at[n]) for n,(x,y) in enumerate(((ccat_any,ccat),(m_any,m),(rcat_any,rcat),(om_any,om),(tv_any,tv),(tu_any,tu)))]
-    for x in moves: x.start()
     rr,cr,tr,kr=rrank[0],crank[0],trank[0,0],krank[0,0]
     i=lax.axis_index("row").astype(jnp.int32); j=lax.axis_index("col").astype(jnp.int32)
+    c=lax.bitwise_and(j,1)*32
+    cmoves=[pltpu.make_async_copy(m_any,m,sems.at[0])]
+    for t in range(16):
+        at=pl.multiple_of(lax.bitwise_xor(i,jnp.int32(FROM[t]))*64,64)
+        cmoves.append(pltpu.make_async_copy(cblocks.at[t],ccat.at[pl.ds(at,64)],sems.at[t+4]))
+    rmoves=[pltpu.make_async_copy(x,y,sems.at[n+1]) for n,(x,y) in enumerate(((om_any,om),(tv_any,tv),(tu_any,tu)))]
+    for t in range(16):
+        rmoves.append(pltpu.make_async_copy(rmine.at[t],rcat.at[pl.ds(pl.multiple_of(64*t+c,32),32)],sems.at[t+20]))
+        rmoves.append(pltpu.make_async_copy(rother.at[t],rcat.at[pl.ds(pl.multiple_of(64*t+32-c,32),32)],sems.at[t+36]))
+    for x in cmoves+rmoves: x.start()
     ru=rcat.at[:,:256]; rv=rcat.at[:,256:]; cu=ccat.at[:,:256]; cv=ccat.at[:,256:]
-    for x in moves[:2]: x.wait()
+    for x in cmoves: x.wait()
     for b in range(4):
         s=slice(256*b,256*b+256); e=256*b+256
         acc=dotg(m[s,:e],cv[:e,:],1,0)
         cw[s,:]=jnp.where(cols(acc.shape,1)<cr,acc,F32(0)).astype(BF)
-    for x in moves[2:]: x.wait()
+    for x in rmoves: x.wait()
     for b in range(4):
         s=slice(256*b,256*b+256); e=256*b+256
         acc=dotg(m[s,:e],rv[:e,:],1,0)
@@ -169,34 +177,53 @@
     plow=dot3(couple,rproj,0,0)
     nv_ref[...]=(pair(tv[...],ptop,1)-pair(cu[...],plow,1)).astype(BF)
 
-def finish(rrank,crank,trank,krank,m,rcat,ccat,tu,tv,om):
+def finish(rrank,crank,trank,krank,m,rmine,rother,cblocks,tu,tv,om):
     smem=pl.BlockSpec(memory_space=pltpu.SMEM); vmem=pl.BlockSpec(memory_space=pltpu.VMEM); far=pl.BlockSpec(memory_space=pl.ANY)
     return pl.pallas_call(finish_kernel,
         out_shape=(jax.ShapeDtypeStruct((32,256),BF),jax.ShapeDtypeStruct((64,256),BF),
                    jax.ShapeDtypeStruct((1024,128),BF),jax.ShapeDtypeStruct((1024,128),BF)),
-        in_specs=[smem]*4+[far]*6,
+        in_specs=[smem]*4+[far]*7,
         out_specs=(vmem,)*4,
         scratch_shapes=[pltpu.VMEM((1024,256),BF)]*2+[pltpu.VMEM((1024,512),BF)]+[pltpu.VMEM((1024,256),BF)]*2
-            +[pltpu.VMEM((1024,128),BF),pltpu.VMEM((1024,1024),BF),pltpu.VMEM((1024,512),BF),pltpu.SemaphoreType.DMA((6,))],
-        compiler_params=pltpu.CompilerParams(vmem_limit_bytes=58*2**20),name="recompress")(rrank,crank,trank,krank,m,rcat,ccat,tu,tv,om)
-
-
-def to_all(block):
+            +[pltpu.VMEM((1024,128),BF),pltpu.VMEM((1024,1024),BF),pltpu.VMEM((1024,512),BF),pltpu.SemaphoreType.DMA((52,))],
+        compiler_params=pltpu.CompilerParams(vmem_limit_bytes=58*2**20),name="recompress")(rrank,crank,trank,krank,m,rmine,rother,cblocks,tu,tv,om)
+
+
+SAME_CORE=[list(range(0,32,2)),list(range(1,32,2))]
+STEPS=(1,3,4,12)
+FROM=[0]
+for _m in STEPS: FROM=FROM+[f^_m for f in FROM]
+
+
+def to_all(block,axis,groups=None):
     every=jnp.broadcast_to(block[None],(16,)+block.shape)
-    return lax.all_to_all(every,"row",split_axis=0,concat_axis=0,tiled=True)
+    return lax.all_to_all(every,axis,split_axis=0,concat_axis=0,axis_index_groups=groups,tiled=True)
+
+
+def other_core(block):
+    return lax.ppermute(block,"col",[(s,s^1) for s in range(32)])
+
+
+def doubled(have,mask):
+    return jnp.concatenate([have,lax.ppermute(have,"row",[(s,s^mask) for s in range(16)])],0)
 
 
 def per_device(diag_tile,row_u,row_v,col_u,col_v,tile_u,tile_v,omega,row_rank,col_rank,tile_rank,keep_rank):
     core=lax.bitwise_and(lax.axis_index("col").astype(jnp.int32),1)
-    rows=jnp.concatenate([row_u[0],row_v[0]],1)
     half=lax.dynamic_slice_in_dim(diag_tile,core*32,32,0)
-    half,rows=lax.optimization_barrier((half,rows))
-    rcat=lax.all_gather(rows,"col",axis=0,tiled=True)
-    mine=to_all(half)
-    other=lax.ppermute(mine,"col",[(s,s^1) for s in range(32)])
-    ccat=to_all(jnp.concatenate([col_u[0],col_v[0]],1)).reshape((1024,512))
+    mine=to_all(half,"row")
+    cblocks=jnp.concatenate([col_u[0],col_v[0]],1)[None]
+    cblocks=doubled(cblocks,STEPS[0])
+    mine,cblocks=lax.optimization_barrier((mine,cblocks))
+    other=other_core(mine)
+    for mask in STEPS[1:3]: cblocks=doubled(cblocks,mask)
+    other,cblocks=lax.optimization_barrier((other,cblocks))
+    cblocks=doubled(cblocks,STEPS[3])
+    rmine=to_all(jnp.concatenate([row_u[0],row_v[0]],1),"col",SAME_CORE)
     strip,inverse=chol(mine,other)
-    row_out,col_out,new_u,new_v=finish(row_rank,col_rank,tile_rank,keep_rank,inverse,rcat,ccat,
+    rmine,inverse=lax.optimization_barrier((rmine,inverse))
+    rother=other_core(rmine)
+    row_out,col_out,new_u,new_v=finish(row_rank,col_rank,tile_rank,keep_rank,inverse,rmine,rother,cblocks,
         tile_u.reshape((1024,256)),tile_v.reshape((1024,256)),omega)
     return (strip,row_out[None],col_out[None],new_u[None,None],new_v[None,None])
 

time: 115 us -> 108 us (0.939)
  starting transfers between devices: 17 us -> 42.9 us
  waiting for transfers between devices: 36 us -> 16.6 us
  between operations: 16.8 us -> 3.62 us
    all_gather x1 -> x0, waiting for transfers between devices: 21.8 us -> none  [per_device(): rcat = lax.all_gather(rows, 'col', axis=0, tiled=True)]
    ppermute x1 -> x6, starting transfers between devices: 5.73 us -> 19.8 us  [the longest x4 10.4 us: doubled(): lax.ppermute(have, 'row', [(s, s ^ mask) for s in range(16)])]
    ppermute x1 -> x6, waiting for transfers between devices: 0.01 us -> 13.5 us  [the longest x4 13.5 us: doubled(): lax.ppermute(have, 'row', [(s, s ^ mask) for s in range(16)])]
    all_to_all x2, starting transfers between devices: 11.2 us -> 23 us  [to_all(): lax.all_to_all(every, axis, split_axis=0, concat_axis=0, axis_index_group...]
    all_to_all x2, waiting for transfers between devices: 13.5 us -> 3.08 us  [to_all(): lax.all_to_all(every, axis, split_axis=0, concat_axis=0, axis_index_group...]
  transfers between devices with their start and end apart: 4 -> 8, of which waited for: 2 -> 3; matrix products, arithmetic and copies ran while one was open for 1% -> 2% of each run, Pallas kernels for 26% -> 27%
where the time goes in v3:
time: 108 us; the launch traced here: 107 us
  starting transfers between devices  42.9 us (40%)
  Pallas kernels  39.6 us (37%)
  waiting for transfers between devices  16.6 us (15%)
  local copies, waits for them, and re-layouts  3.65 us (3%)
  between operations  3.62 us (3%)
  other arithmetic  1.17 us (1%)
    pallas_call x1, Pallas kernels, chol(): pl.pallas_call(chol_kernel, out_shape=(jax.ShapeDtypeStruct((64, 1024), F...  29.4 us
    all_to_all x2, starting transfers between devices, to_all(): lax.all_to_all(every, axis, split_axis=0, concat_axis=0, axis_index_group...  23 us
    ppermute x4, waiting for transfers between devices, doubled(): lax.ppermute(have, 'row', [(s, s ^ mask) for s in range(16)])  13.5 us
    ppermute x4, starting transfers between devices, doubled(): lax.ppermute(have, 'row', [(s, s ^ mask) for s in range(16)])  10.4 us
    pallas_call x1, Pallas kernels, finish(): pl.pallas_call(finish_kernel, out_shape=(jax.ShapeDtypeStruct((32, 256),...  10.3 us
    ppermute x2, starting transfers between devices, other_core(): return lax.ppermute(block, 'col', [(s, s ^ 1) for s in range(32)])  9.48 us
    all_to_all x2, waiting for transfers between devices, to_all(): lax.all_to_all(every, axis, split_axis=0, concat_axis=0, axis_index_group...  3.08 us
  transfers between devices with their start and end apart: 8, of which 3 were waited for; matrix products, arithmetic and copies ran while one was open for 2% of the time, Pallas kernels for 27%

profile of v3, /device:TPU:1, one launch (start us, length us, event | category | flops | bytes accessed | tf_op | source)
XLA Modules:
  0.0 107.5 jit_solution(11060341117673680439)
XLA Ops:
  0.6 0.0 copy-start
  0.6 0.0 copy-start.5
  0.7 0.0 copy-start.4
  0.7 0.9 copy-done
  1.5 0.0 copy-start.6
  1.6 0.0 copy-start.7
  1.6 1.1 %broadcast_in_dim.27 = bf16[16,32,1024]{2,1,0:T(8,128)(2,1)} broadcast(bf16[32,1024]{1,0:T(8,128)(2,1)S(1)} %constant_dynamic-slice_fusion), dimensions={1,2} | broadcast | bytes 1114112 | tf_op jit(solution)/shard_map/broadcast_in_dim | solution.py:199
  2.7 7.6 %all-to-all-start = ((bf16[16,32,1024]{2,1,0:T(8,128)(2,1)}), bf16[16,32,1024]{2,1,0:T(8,128)(2,1)S(1)}, u32[]{:S(2)}, u32[]{:S(2)}) async-start(bf16[16,32,1024]{2,1,0:T(8,128)(2,1)} %broadcast_in_dim.27), calls=%async_computation | async-start | bytes 2097152 | tf_op jit(solution)/shard_map/all_to_all | solution.py:200
  10.3 0.0 copy-done.5
  10.3 0.0 copy-done.4
  10.3 3.3 %collective-permute-start = (bf16[1,64,512]{2,1,0:T(8,128)(2,1)S(1)}, bf16[1,64,512]{2,1,0:T(8,128)(2,1)S(1)}, u32[]{:S(2)}, u32[]{:S(2)}) collective-permute-start(bf16[1,64,512]{2,1,0:T(8,128)(2,1)S(1)} %maximum_bitcast_fusion), channel_id=1, source_target_pairs={{0,32},{32,0},{64,96},{96,64},{128,160},{160,128},{192,224},{224,1... | collective-permute-start | bytes 196616 | tf_op jit(solution)/shard_map/ppermute | solution.py:208
  13.6 7.9 %collective-permute-done = bf16[1,64,512]{2,1,0:T(8,128)(2,1)S(1)} collective-permute-done((bf16[1,64,512]{2,1,0:T(8,128)(2,1)S(1)}, bf16[1,64,512]{2,1,0:T(8,128)(2,1)S(1)}, u32[]{:S(2)}, u32[]{:S(2)}) %collective-permute-start) | collective-permute-done | bytes 65568 | tf_op jit(solution)/shard_map/ppermute | solution.py:208
  21.4 3.1 %all-to-all-done.mine_any = bf16[16,32,1024]{2,1,0:T(8,128)(2,1)S(1)} async-done(((bf16[16,32,1024]{2,1,0:T(8,128)(2,1)}), bf16[16,32,1024]{2,1,0:T(8,128)(2,1)S(1)}, u32[]{:S(2)}, u32[]{:S(2)}) %all-to-all-start) | async-done | bytes 1048608 | tf_op jit(solution)/shard_map/all_to_all | solution.py:200
  24.5 0.0 copy-start.2
  24.5 5.7 %collective-permute-start.1 = (bf16[16,32,1024]{2,1,0:T(8,128)(2,1)S(1)}, bf16[16,32,1024]{2,1,0:T(8,128)(2,1)}, u32[]{:S(2)}, u32[]{:S(2)}) collective-permute-start(bf16[16,32,1024]{2,1,0:T(8,128)(2,1)S(1)} %all-to-all-done.mine_any), channel_id=1, source_target_pairs={{0,1},{1,0},{2,3},{3,2},{4,5},{5,4},{6,7},{7,6},{8,9},{9,8},{10,11... | collective-permute-start | bytes 3145736 | tf_op jit(solution)/shard_map/ppermute | solution.py:204
  30.3 2.6 %collective-permute-start.2 = (bf16[2,64,512]{2,1,0:T(8,128)(2,1)S(1)}, bf16[2,64,512]{2,1,0:T(8,128)(2,1)S(1)}, u32[]{:S(2)}, u32[]{:S(2)}) collective-permute-start(bf16[2,64,512]{2,1,0:T(8,128)(2,1)S(1)} %pad_maximum_fusion.3), channel_id=1, source_target_pairs={{0,96},{32,64},{64,32},{96,0},{128,224},{160,192},{192,160},{224,1... | collective-permute-start | bytes 393224 | tf_op jit(solution)/shard_map/ppermute | solution.py:208
  32.9 5.6 %collective-permute-done.2 = bf16[2,64,512]{2,1,0:T(8,128)(2,1)S(1)} collective-permute-done((bf16[2,64,512]{2,1,0:T(8,128)(2,1)S(1)}, bf16[2,64,512]{2,1,0:T(8,128)(2,1)S(1)}, u32[]{:S(2)}, u32[]{:S(2)}) %collective-permute-start.2) | collective-permute-done | bytes 131104 | tf_op jit(solution)/shard_map/ppermute | solution.py:208
  38.5 1.9 %collective-permute-start.3 = (bf16[4,64,512]{2,1,0:T(8,128)(2,1)S(1)}, bf16[4,64,512]{2,1,0:T(8,128)(2,1)S(1)}, u32[]{:S(2)}, u32[]{:S(2)}) collective-permute-start(bf16[4,64,512]{2,1,0:T(8,128)(2,1)S(1)} %pad_maximum_fusion.2), channel_id=1, source_target_pairs={{0,128},{32,160},{64,192},{96,224},{128,0},{160,32},{192,64},{224,... | collective-permute-start | bytes 786440 | tf_op jit(solution)/shard_map/ppermute | solution.py:208
  40.5 0.0 copy-done.6
  40.5 0.0 copy-done.7
  40.5 0.8 broadcast_in_dim.29
  41.3 15.4 %all-to-all-start.1 = ((bf16[16,32,512]{2,1,0:T(8,128)(2,1)}), bf16[16,32,512]{2,1,0:T(8,128)(2,1)S(1)}, u32[]{:S(2)}, u32[]{:S(2)}) async-start(bf16[16,32,512]{2,1,0:T(8,128)(2,1)} %broadcast_in_dim.29), calls=%async_computation.1 | async-start | bytes 1048576 | tf_op jit(solution)/shard_map/all_to_all | solution.py:200
  56.8 0.0 collective-permute-done.3
  56.8 0.1 pad_maximum_fusion.1
  56.9 0.0 collective-permute-done.1.other_any
  56.9 2.6 %collective-permute-start.5 = (bf16[8,64,512]{2,1,0:T(8,128)(2,1)S(1)}, bf16[8,64,512]{2,1,0:T(8,128)(2,1)S(1)}, u32[]{:S(2)}, u32[]{:S(2)}) collective-permute-start(bf16[8,64,512]{2,1,0:T(8,128)(2,1)S(1)} %pad_maximum_fusion.1), channel_id=1, source_target_pairs={{0,384},{32,416},{64,448},{96,480},{128,256},{160,288},{192,320},{... | collective-permute-start | bytes 1572872 | tf_op jit(solution)/shard_map/ppermute | solution.py:208
  59.4 0.0 copy-done.2
  59.5 29.4 %chol_inverse.1 = (f32[64,1024]{1,0:T(8,128)}, bf16[1024,1024]{1,0:T(8,128)(2,1)}) custom-call(bf16[16,32,1024]{2,1,0:T(8,128)(2,1)} %copy-done.2, bf16[16,32,1024]{2,1,0:T(8,128)(2,1)} %collective-permute-done.1.other_any), custom_call_target="tpu_custom_call" | custom-call | flops 30000001024 | bytes 5000000 | tf_op jit(solution)/shard_map/chol_inverse/pallas_call | solution.py:115
  88.8 0.0 all-to-all-done.1.rmine
  88.8 0.0 copy-start.1
  88.8 3.7 %collective-permute-start.4 = (bf16[16,32,512]{2,1,0:T(8,128)(2,1)S(1)}, bf16[16,32,512]{2,1,0:T(8,128)(2,1)S(1)}, u32[]{:S(2)}, u32[]{:S(2)}) collective-permute-start(bf16[16,32,512]{2,1,0:T(8,128)(2,1)S(1)} %all-to-all-done.1.rmine), channel_id=1, source_target_pairs={{0,1},{1,0},{2,3},{3,2},{4,5},{5,4},{6,7},{7,6},{8,9},{9,8},{10,11... | collective-permute-start | bytes 1572872 | tf_op jit(solution)/shard_map/ppermute | solution.py:204
  95.2 0.0 collective-permute-done.5
  95.2 1.1 pad_maximum_fusion.cblocks
  96.2 0.0 collective-permute-done.4.rother
  96.2 0.0 copy-start.3
  96.3 0.0 copy-done.1
  96.3 0.8 copy-done.3
  97.0 10.3 %recompress.1 = (bf16[32,256]{1,0:T(8,128)(2,1)}, bf16[64,256]{1,0:T(8,128)(2,1)}, bf16[1024,128]{1,0:T(8,128)(2,1)}, bf16[1024,128]{1,0:T(8,128)(2,1)}) custom-call(s32[1]{0:T(128)S(6)} %copy.17.rrank, s32[1]{0:T(128)S(6)} %copy.18.crank, s32[1,1]{1,0:T(1,128)S(6)} %copy.19.trank, s32[1,1]{1,0:T(1,128)S(6)} %copy.20.krank, ...), custom_call_target="tpu_custom_call" | custom-call | tf_op jit(solution)/shard_map/recompress/pallas_call | solution.py:182
  (5 shorter events, 0.1 us)
Async XLA Ops:
  0.6 0.9 copy-start
  0.6 9.6 %copy-start.5 = (bf16[1,64,256]{2,1,0:T(8,128)(2,1)S(1)}, bf16[1,64,256]{2,1,0:T(8,128)(2,1)}, u32[]{:S(2)}) copy-start(bf16[1,64,256]{2,1,0:T(8,128)(2,1)} %param.15) | copy-start | bytes 98308
  0.7 9.6 %copy-start.4 = (bf16[1,64,256]{2,1,0:T(8,128)(2,1)S(1)}, bf16[1,64,256]{2,1,0:T(8,128)(2,1)}, u32[]{:S(2)}) copy-start(bf16[1,64,256]{2,1,0:T(8,128)(2,1)} %param.16) | copy-start | bytes 98308
  1.5 38.9 %copy-start.6 = (bf16[1,32,256]{2,1,0:T(8,128)(2,1)S(1)}, bf16[1,32,256]{2,1,0:T(8,128)(2,1)}, u32[]{:S(2)}) copy-start(bf16[1,32,256]{2,1,0:T(8,128)(2,1)} %param.14) | copy-start | bytes 49156
  1.6 38.9 %copy-start.7 = (bf16[1,32,256]{2,1,0:T(8,128)(2,1)S(1)}, bf16[1,32,256]{2,1,0:T(8,128)(2,1)}, u32[]{:S(2)}) copy-start(bf16[1,32,256]{2,1,0:T(8,128)(2,1)} %param.13) | copy-start | bytes 49156
  2.7 21.9 %all-to-all-start = ((bf16[16,32,1024]{2,1,0:T(8,128)(2,1)}), bf16[16,32,1024]{2,1,0:T(8,128)(2,1)S(1)}, u32[]{:S(2)}, u32[]{:S(2)}) async-start(bf16[16,32,1024]{2,1,0:T(8,128)(2,1)} %broadcast_in_dim.27), calls=%async_computation | async-start | bytes 2097152 | tf_op jit(solution)/shard_map/all_to_all | solution.py:200
  10.3 11.1 %collective-permute-start = (bf16[1,64,512]{2,1,0:T(8,128)(2,1)S(1)}, bf16[1,64,512]{2,1,0:T(8,128)(2,1)S(1)}, u32[]{:S(2)}, u32[]{:S(2)}) collective-permute-start(bf16[1,64,512]{2,1,0:T(8,128)(2,1)S(1)} %maximum_bitcast_fusion), channel_id=1, source_target_pairs={{0,32},{32,0},{64,96},{96,64},{128,160},{160,128},{192,224},{224,1... | collective-permute-start | bytes 196616 | tf_op jit(solution)/shard_map/ppermute | solution.py:208
  24.5 34.9 %copy-start.2 = (bf16[16,32,1024]{2,1,0:T(8,128)(2,1)}, bf16[16,32,1024]{2,1,0:T(8,128)(2,1)S(1)}, u32[]{:S(2)}) copy-start(bf16[16,32,1024]{2,1,0:T(8,128)(2,1)S(1)} %all-to-all-done.mine_any) | copy-start | bytes 3145732
  24.5 32.3 %collective-permute-start.1 = (bf16[16,32,1024]{2,1,0:T(8,128)(2,1)S(1)}, bf16[16,32,1024]{2,1,0:T(8,128)(2,1)}, u32[]{:S(2)}, u32[]{:S(2)}) collective-permute-start(bf16[16,32,1024]{2,1,0:T(8,128)(2,1)S(1)} %all-to-all-done.mine_any), channel_id=1, source_target_pairs={{0,1},{1,0},{2,3},{3,2},{4,5},{5,4},{6,7},{7,6},{8,9},{9,8},{10,11... | collective-permute-start | bytes 3145736 | tf_op jit(solution)/shard_map/ppermute | solution.py:204
  30.3 8.2 %collective-permute-start.2 = (bf16[2,64,512]{2,1,0:T(8,128)(2,1)S(1)}, bf16[2,64,512]{2,1,0:T(8,128)(2,1)S(1)}, u32[]{:S(2)}, u32[]{:S(2)}) collective-permute-start(bf16[2,64,512]{2,1,0:T(8,128)(2,1)S(1)} %pad_maximum_fusion.3), channel_id=1, source_target_pairs={{0,96},{32,64},{64,32},{96,0},{128,224},{160,192},{192,160},{224,1... | collective-permute-start | bytes 393224 | tf_op jit(solution)/shard_map/ppermute | solution.py:208
  38.5 18.3 %collective-permute-start.3 = (bf16[4,64,512]{2,1,0:T(8,128)(2,1)S(1)}, bf16[4,64,512]{2,1,0:T(8,128)(2,1)S(1)}, u32[]{:S(2)}, u32[]{:S(2)}) collective-permute-start(bf16[4,64,512]{2,1,0:T(8,128)(2,1)S(1)} %pad_maximum_fusion.2), channel_id=1, source_target_pairs={{0,128},{32,160},{64,192},{96,224},{128,0},{160,32},{192,64},{224,... | collective-permute-start | bytes 786440 | tf_op jit(solution)/shard_map/ppermute | solution.py:208
  41.3 47.5 %all-to-all-start.1 = ((bf16[16,32,512]{2,1,0:T(8,128)(2,1)}), bf16[16,32,512]{2,1,0:T(8,128)(2,1)S(1)}, u32[]{:S(2)}, u32[]{:S(2)}) async-start(bf16[16,32,512]{2,1,0:T(8,128)(2,1)} %broadcast_in_dim.29), calls=%async_computation.1 | async-start | bytes 1048576 | tf_op jit(solution)/shard_map/all_to_all | solution.py:200
  56.9 38.3 %collective-permute-start.5 = (bf16[8,64,512]{2,1,0:T(8,128)(2,1)S(1)}, bf16[8,64,512]{2,1,0:T(8,128)(2,1)S(1)}, u32[]{:S(2)}, u32[]{:S(2)}) collective-permute-start(bf16[8,64,512]{2,1,0:T(8,128)(2,1)S(1)} %pad_maximum_fusion.1), channel_id=1, source_target_pairs={{0,384},{32,416},{64,448},{96,480},{128,256},{160,288},{192,320},{... | collective-permute-start | bytes 1572872 | tf_op jit(solution)/shard_map/ppermute | solution.py:208
  88.8 7.4 %copy-start.1 = (bf16[16,32,512]{2,1,0:T(8,128)(2,1)}, bf16[16,32,512]{2,1,0:T(8,128)(2,1)S(1)}, u32[]{:S(2)}) copy-start(bf16[16,32,512]{2,1,0:T(8,128)(2,1)S(1)} %all-to-all-done.1.rmine) | copy-start | bytes 1572868
  88.8 7.4 %collective-permute-start.4 = (bf16[16,32,512]{2,1,0:T(8,128)(2,1)S(1)}, bf16[16,32,512]{2,1,0:T(8,128)(2,1)S(1)}, u32[]{:S(2)}, u32[]{:S(2)}) collective-permute-start(bf16[16,32,512]{2,1,0:T(8,128)(2,1)S(1)} %all-to-all-done.1.rmine), channel_id=1, source_target_pairs={{0,1},{1,0},{2,3},{3,2},{4,5},{5,4},{6,7},{7,6},{8,9},{9,8},{10,11... | collective-permute-start | bytes 1572872 | tf_op jit(solution)/shard_map/ppermute | solution.py:204
  96.2 0.8 copy-start.3

commit v4 on v3

--- a/solution.py
+++ b/solution.py
@@ -129,7 +129,7 @@
     both=dotg(a,jnp.concatenate([h,l],1),ca,0)
     return both[:,:n]+both[:,n:]
 
-def finish_kernel(rrank,crank,trank,krank,m_any,rmine,rother,cblocks,tu_any,tv_any,om_any,row_ref,col_ref,nu_ref,nv_ref,
+def finish_kernel(rrank,crank,trank,krank,m_any,rmine,rother,cfirst,clast,tu_any,tv_any,om_any,row_ref,col_ref,nu_ref,nv_ref,
                   rw,cw,rcat,tu,tv,om,m,ccat,sems):
     rr,cr,tr,kr=rrank[0],crank[0],trank[0,0],krank[0,0]
     i=lax.axis_index("row").astype(jnp.int32); j=lax.axis_index("col").astype(jnp.int32)
@@ -137,7 +137,7 @@
     cmoves=[pltpu.make_async_copy(m_any,m,sems.at[0])]
     for t in range(16):
         at=pl.multiple_of(lax.bitwise_xor(i,jnp.int32(FROM[t]))*64,64)
-        cmoves.append(pltpu.make_async_copy(cblocks.at[t],ccat.at[pl.ds(at,64)],sems.at[t+4]))
+        cmoves.append(pltpu.make_async_copy((cfirst if t<8 else clast).at[t%8],ccat.at[pl.ds(at,64)],sems.at[t+4]))
     rmoves=[pltpu.make_async_copy(x,y,sems.at[n+1]) for n,(x,y) in enumerate(((om_any,om),(tv_any,tv),(tu_any,tu)))]
     for t in range(16):
         rmoves.append(pltpu.make_async_copy(rmine.at[t],rcat.at[pl.ds(pl.multiple_of(64*t+c,32),32)],sems.at[t+20]))
@@ -177,16 +177,16 @@
     plow=dot3(couple,rproj,0,0)
     nv_ref[...]=(pair(tv[...],ptop,1)-pair(cu[...],plow,1)).astype(BF)
 
-def finish(rrank,crank,trank,krank,m,rmine,rother,cblocks,tu,tv,om):
+def finish(rrank,crank,trank,krank,m,rmine,rother,cfirst,clast,tu,tv,om):
     smem=pl.BlockSpec(memory_space=pltpu.SMEM); vmem=pl.BlockSpec(memory_space=pltpu.VMEM); far=pl.BlockSpec(memory_space=pl.ANY)
     return pl.pallas_call(finish_kernel,
         out_shape=(jax.ShapeDtypeStruct((32,256),BF),jax.ShapeDtypeStruct((64,256),BF),
                    jax.ShapeDtypeStruct((1024,128),BF),jax.ShapeDtypeStruct((1024,128),BF)),
-        in_specs=[smem]*4+[far]*7,
+        in_specs=[smem]*4+[far]*8,
         out_specs=(vmem,)*4,
         scratch_shapes=[pltpu.VMEM((1024,256),BF)]*2+[pltpu.VMEM((1024,512),BF)]+[pltpu.VMEM((1024,256),BF)]*2
             +[pltpu.VMEM((1024,128),BF),pltpu.VMEM((1024,1024),BF),pltpu.VMEM((1024,512),BF),pltpu.SemaphoreType.DMA((52,))],
-        compiler_params=pltpu.CompilerParams(vmem_limit_bytes=58*2**20),name="recompress")(rrank,crank,trank,krank,m,rmine,rother,cblocks,tu,tv,om)
+        compiler_params=pltpu.CompilerParams(vmem_limit_bytes=58*2**20),name="recompress")(rrank,crank,trank,krank,m,rmine,rother,cfirst,clast,tu,tv,om)
 
 
 SAME_CORE=[list(range(0,32,2)),list(range(1,32,2))]
@@ -204,8 +204,12 @@
     return lax.ppermute(block,"col",[(s,s^1) for s in range(32)])
 
 
+def exchanged(have,mask):
+    return lax.ppermute(have,"row",[(s,s^mask) for s in range(16)])
+
+
 def doubled(have,mask):
-    return jnp.concatenate([have,lax.ppermute(have,"row",[(s,s^mask) for s in range(16)])],0)
+    return jnp.concatenate([have,exchanged(have,mask)],0)
 
 
 def per_device(diag_tile,row_u,row_v,col_u,col_v,tile_u,tile_v,omega,row_rank,col_rank,tile_rank,keep_rank):
@@ -218,12 +222,12 @@
     other=other_core(mine)
     for mask in STEPS[1:3]: cblocks=doubled(cblocks,mask)
     other,cblocks=lax.optimization_barrier((other,cblocks))
-    cblocks=doubled(cblocks,STEPS[3])
+    clast=exchanged(cblocks,STEPS[3])
     rmine=to_all(jnp.concatenate([row_u[0],row_v[0]],1),"col",SAME_CORE)
     strip,inverse=chol(mine,other)
-    rmine,inverse=lax.optimization_barrier((rmine,inverse))
+    rmine,inverse,clast=lax.optimization_barrier((rmine,inverse,clast))
     rother=other_core(rmine)
-    row_out,col_out,new_u,new_v=finish(row_rank,col_rank,tile_rank,keep_rank,inverse,rmine,rother,cblocks,
+    row_out,col_out,new_u,new_v=finish(row_rank,col_rank,tile_rank,keep_rank,inverse,rmine,rother,cblocks,clast,
         tile_u.reshape((1024,256)),tile_v.reshape((1024,256)),omega)
     return (strip,row_out[None],col_out[None],new_u[None,None],new_v[None,None])
 

time: 108 us -> 107 us (level)
  transfers between devices with their start and end apart: 8 -> 8, of which waited for: 3 -> 3; matrix products, arithmetic and copies ran while one was open for 2% -> 1% of each run, Pallas kernels for 27% -> 28%
where the time goes in v4:
time: 107 us; the launch traced here: 106 us
  starting transfers between devices  42.9 us (40%)
  Pallas kernels  39.6 us (37%)
  waiting for transfers between devices  16.6 us (16%)
  between operations  3.67 us (3%)
  local copies, waits for them, and re-layouts  3.63 us (3%)
    pallas_call x1, Pallas kernels, chol(): pl.pallas_call(chol_kernel, out_shape=(jax.ShapeDtypeStruct((64, 1024), F...  29.3 us
    all_to_all x2, starting transfers between devices, to_all(): lax.all_to_all(every, axis, split_axis=0, concat_axis=0, axis_index_group...  23 us
    ppermute x4, waiting for transfers between devices, exchanged(): return lax.ppermute(have, 'row', [(s, s ^ mask) for s in range(16)])  13.5 us
    ppermute x4, starting transfers between devices, exchanged(): return lax.ppermute(have, 'row', [(s, s ^ mask) for s in range(16)])  10.3 us
    pallas_call x1, Pallas kernels, finish(): pl.pallas_call(finish_kernel, out_shape=(jax.ShapeDtypeStruct((32, 256),...  10.3 us
    ppermute x2, starting transfers between devices, other_core(): return lax.ppermute(block, 'col', [(s, s ^ 1) for s in range(32)])  9.51 us
    all_to_all x2, waiting for transfers between devices, to_all(): lax.all_to_all(every, axis, split_axis=0, concat_axis=0, axis_index_group...  3.08 us
  transfers between devices with their start and end apart: 8, of which 3 were waited for; matrix products, arithmetic and copies ran while one was open for 1% of the time, Pallas kernels for 28%

profile of v4, /device:TPU:1, one launch (start us, length us, event | category | flops | bytes accessed | tf_op | source)
XLA Modules:
  0.0 106.5 jit_solution(1637883392010745012)
XLA Ops:
  0.6 0.0 copy-start
  0.6 0.0 copy-start.6
  0.7 0.0 copy-start.7
  0.7 0.9 copy-done
  1.5 0.0 copy-start.8
  1.6 0.0 copy-start.9
  1.6 1.1 %broadcast_in_dim.27 = bf16[16,32,1024]{2,1,0:T(8,128)(2,1)} broadcast(bf16[32,1024]{1,0:T(8,128)(2,1)S(1)} %constant_dynamic-slice_fusion), dimensions={1,2} | broadcast | bytes 1114112 | tf_op jit(solution)/shard_map/broadcast_in_dim | solution.py:199
  2.7 7.6 %all-to-all-start = ((bf16[16,32,1024]{2,1,0:T(8,128)(2,1)}), bf16[16,32,1024]{2,1,0:T(8,128)(2,1)S(1)}, u32[]{:S(2)}, u32[]{:S(2)}) async-start(bf16[16,32,1024]{2,1,0:T(8,128)(2,1)} %broadcast_in_dim.27), calls=%async_computation | async-start | bytes 2097152 | tf_op jit(solution)/shard_map/all_to_all | solution.py:200
  10.3 0.0 copy-done.6
  10.3 0.0 copy-done.7
  10.3 3.3 %collective-permute-start = (bf16[1,64,512]{2,1,0:T(8,128)(2,1)S(1)}, bf16[1,64,512]{2,1,0:T(8,128)(2,1)S(1)}, u32[]{:S(2)}, u32[]{:S(2)}) collective-permute-start(bf16[1,64,512]{2,1,0:T(8,128)(2,1)S(1)} %maximum_bitcast_fusion), channel_id=1, source_target_pairs={{0,32},{32,0},{64,96},{96,64},{128,160},{160,128},{192,224},{224,1... | collective-permute-start | bytes 196616 | tf_op jit(solution)/shard_map/ppermute | solution.py:208
  13.6 7.9 %collective-permute-done = bf16[1,64,512]{2,1,0:T(8,128)(2,1)S(1)} collective-permute-done((bf16[1,64,512]{2,1,0:T(8,128)(2,1)S(1)}, bf16[1,64,512]{2,1,0:T(8,128)(2,1)S(1)}, u32[]{:S(2)}, u32[]{:S(2)}) %collective-permute-start) | collective-permute-done | bytes 65568 | tf_op jit(solution)/shard_map/ppermute | solution.py:208
  21.5 3.1 %all-to-all-done.mine_any = bf16[16,32,1024]{2,1,0:T(8,128)(2,1)S(1)} async-done(((bf16[16,32,1024]{2,1,0:T(8,128)(2,1)}), bf16[16,32,1024]{2,1,0:T(8,128)(2,1)S(1)}, u32[]{:S(2)}, u32[]{:S(2)}) %all-to-all-start) | async-done | bytes 1048608 | tf_op jit(solution)/shard_map/all_to_all | solution.py:200
  24.5 0.0 copy-start.3
  24.5 5.7 %collective-permute-start.1 = (bf16[16,32,1024]{2,1,0:T(8,128)(2,1)S(1)}, bf16[16,32,1024]{2,1,0:T(8,128)(2,1)}, u32[]{:S(2)}, u32[]{:S(2)}) collective-permute-start(bf16[16,32,1024]{2,1,0:T(8,128)(2,1)S(1)} %all-to-all-done.mine_any), channel_id=1, source_target_pairs={{0,1},{1,0},{2,3},{3,2},{4,5},{5,4},{6,7},{7,6},{8,9},{9,8},{10,11... | collective-permute-start | bytes 3145736 | tf_op jit(solution)/shard_map/ppermute | solution.py:204
  30.3 2.6 %collective-permute-start.2 = (bf16[2,64,512]{2,1,0:T(8,128)(2,1)S(1)}, bf16[2,64,512]{2,1,0:T(8,128)(2,1)S(1)}, u32[]{:S(2)}, u32[]{:S(2)}) collective-permute-start(bf16[2,64,512]{2,1,0:T(8,128)(2,1)S(1)} %pad_maximum_fusion.2), channel_id=1, source_target_pairs={{0,96},{32,64},{64,32},{96,0},{128,224},{160,192},{192,160},{224,1... | collective-permute-start | bytes 393224 | tf_op jit(solution)/shard_map/ppermute | solution.py:208
  32.9 5.6 %collective-permute-done.2 = bf16[2,64,512]{2,1,0:T(8,128)(2,1)S(1)} collective-permute-done((bf16[2,64,512]{2,1,0:T(8,128)(2,1)S(1)}, bf16[2,64,512]{2,1,0:T(8,128)(2,1)S(1)}, u32[]{:S(2)}, u32[]{:S(2)}) %collective-permute-start.2) | collective-permute-done | bytes 131104 | tf_op jit(solution)/shard_map/ppermute | solution.py:208
  38.5 1.9 %collective-permute-start.3 = (bf16[4,64,512]{2,1,0:T(8,128)(2,1)S(1)}, bf16[4,64,512]{2,1,0:T(8,128)(2,1)S(1)}, u32[]{:S(2)}, u32[]{:S(2)}) collective-permute-start(bf16[4,64,512]{2,1,0:T(8,128)(2,1)S(1)} %pad_maximum_fusion.1), channel_id=1, source_target_pairs={{0,128},{32,160},{64,192},{96,224},{128,0},{160,32},{192,64},{224,... | collective-permute-start | bytes 786440 | tf_op jit(solution)/shard_map/ppermute | solution.py:208
  40.5 0.0 copy-done.8
  40.5 0.0 copy-done.9
  40.5 0.8 broadcast_in_dim.29
  41.3 15.4 %all-to-all-start.1 = ((bf16[16,32,512]{2,1,0:T(8,128)(2,1)}), bf16[16,32,512]{2,1,0:T(8,128)(2,1)S(1)}, u32[]{:S(2)}, u32[]{:S(2)}) async-start(bf16[16,32,512]{2,1,0:T(8,128)(2,1)} %broadcast_in_dim.29), calls=%async_computation.1 | async-start | bytes 1048576 | tf_op jit(solution)/shard_map/all_to_all | solution.py:200
  56.8 0.0 collective-permute-done.3
  56.8 0.1 pad_maximum_fusion.cfirst
  56.9 0.0 copy-start.2
  56.9 0.0 collective-permute-done.1.other_any
  56.9 2.6 %collective-permute-start.4 = (bf16[8,64,512]{2,1,0:T(8,128)(2,1)S(1)}, bf16[8,64,512]{2,1,0:T(8,128)(2,1)S(1)}, u32[]{:S(2)}, u32[]{:S(2)}) collective-permute-start(bf16[8,64,512]{2,1,0:T(8,128)(2,1)S(1)} %pad_maximum_fusion.cfirst), channel_id=1, source_target_pairs={{0,384},{32,416},{64,448},{96,480},{128,256},{160,288},{192,320},{... | collective-permute-start | bytes 1572872 | tf_op jit(solution)/shard_map/ppermute | solution.py:208
  59.5 0.0 copy-done.3
  59.5 29.3 %chol_inverse.1 = (f32[64,1024]{1,0:T(8,128)}, bf16[1024,1024]{1,0:T(8,128)(2,1)}) custom-call(bf16[16,32,1024]{2,1,0:T(8,128)(2,1)} %copy-done.3, bf16[16,32,1024]{2,1,0:T(8,128)(2,1)} %collective-permute-done.1.other_any), custom_call_target="tpu_custom_call" | custom-call | flops 30000001024 | bytes 5000000 | tf_op jit(solution)/shard_map/chol_inverse/pallas_call | solution.py:115
  88.8 0.0 copy-done.2
  88.8 0.0 all-to-all-done.1.rmine
  88.8 0.0 copy-start.1
  88.8 0.0 collective-permute-done.4.clast
  88.8 0.0 copy-start.4
  88.9 3.8 %collective-permute-start.5 = (bf16[16,32,512]{2,1,0:T(8,128)(2,1)S(1)}, bf16[16,32,512]{2,1,0:T(8,128)(2,1)S(1)}, u32[]{:S(2)}, u32[]{:S(2)}) collective-permute-start(bf16[16,32,512]{2,1,0:T(8,128)(2,1)S(1)} %all-to-all-done.1.rmine), channel_id=1, source_target_pairs={{0,1},{1,0},{2,3},{3,2},{4,5},{5,4},{6,7},{7,6},{8,9},{9,8},{10,11... | collective-permute-start | bytes 1572872 | tf_op jit(solution)/shard_map/ppermute | solution.py:204
  95.2 0.0 collective-permute-done.5.rother
  95.2 0.0 copy-start.5
  95.2 0.0 copy-done.1
  95.2 0.0 copy-done.4
  95.3 0.8 copy-done.5
  96.0 10.3 %recompress.1 = (bf16[32,256]{1,0:T(8,128)(2,1)}, bf16[64,256]{1,0:T(8,128)(2,1)}, bf16[1024,128]{1,0:T(8,128)(2,1)}, bf16[1024,128]{1,0:T(8,128)(2,1)}) custom-call(s32[1]{0:T(128)S(6)} %copy.17.rrank, s32[1]{0:T(128)S(6)} %copy.18.crank, s32[1,1]{1,0:T(1,128)S(6)} %copy.19.trank, s32[1,1]{1,0:T(1,128)S(6)} %copy.20.krank, ...), custom_call_target="tpu_custom_call" | custom-call | tf_op jit(solution)/shard_map/recompress/pallas_call | solution.py:182
  (5 shorter events, 0.1 us)
Async XLA Ops:
  0.6 0.9 copy-start
  0.6 9.6 %copy-start.6 = (bf16[1,64,256]{2,1,0:T(8,128)(2,1)S(1)}, bf16[1,64,256]{2,1,0:T(8,128)(2,1)}, u32[]{:S(2)}) copy-start(bf16[1,64,256]{2,1,0:T(8,128)(2,1)} %param.16) | copy-start | bytes 98308
  0.7 9.6 %copy-start.7 = (bf16[1,64,256]{2,1,0:T(8,128)(2,1)S(1)}, bf16[1,64,256]{2,1,0:T(8,128)(2,1)}, u32[]{:S(2)}) copy-start(bf16[1,64,256]{2,1,0:T(8,128)(2,1)} %param.15) | copy-start | bytes 98308
  1.5 38.9 %copy-start.8 = (bf16[1,32,256]{2,1,0:T(8,128)(2,1)S(1)}, bf16[1,32,256]{2,1,0:T(8,128)(2,1)}, u32[]{:S(2)}) copy-start(bf16[1,32,256]{2,1,0:T(8,128)(2,1)} %param.14) | copy-start | bytes 49156
  1.6 38.9 %copy-start.9 = (bf16[1,32,256]{2,1,0:T(8,128)(2,1)S(1)}, bf16[1,32,256]{2,1,0:T(8,128)(2,1)}, u32[]{:S(2)}) copy-start(bf16[1,32,256]{2,1,0:T(8,128)(2,1)} %param.13) | copy-start | bytes 49156
  2.7 21.9 %all-to-all-start = ((bf16[16,32,1024]{2,1,0:T(8,128)(2,1)}), bf16[16,32,1024]{2,1,0:T(8,128)(2,1)S(1)}, u32[]{:S(2)}, u32[]{:S(2)}) async-start(bf16[16,32,1024]{2,1,0:T(8,128)(2,1)} %broadcast_in_dim.27), calls=%async_computation | async-start | bytes 2097152 | tf_op jit(solution)/shard_map/all_to_all | solution.py:200
  10.3 11.1 %collective-permute-start = (bf16[1,64,512]{2,1,0:T(8,128)(2,1)S(1)}, bf16[1,64,512]{2,1,0:T(8,128)(2,1)S(1)}, u32[]{:S(2)}, u32[]{:S(2)}) collective-permute-start(bf16[1,64,512]{2,1,0:T(8,128)(2,1)S(1)} %maximum_bitcast_fusion), channel_id=1, source_target_pairs={{0,32},{32,0},{64,96},{96,64},{128,160},{160,128},{192,224},{224,1... | collective-permute-start | bytes 196616 | tf_op jit(solution)/shard_map/ppermute | solution.py:208
  24.5 34.9 %copy-start.3 = (bf16[16,32,1024]{2,1,0:T(8,128)(2,1)}, bf16[16,32,1024]{2,1,0:T(8,128)(2,1)S(1)}, u32[]{:S(2)}) copy-start(bf16[16,32,1024]{2,1,0:T(8,128)(2,1)S(1)} %all-to-all-done.mine_any) | copy-start | bytes 3145732
  24.5 32.3 %collective-permute-start.1 = (bf16[16,32,1024]{2,1,0:T(8,128)(2,1)S(1)}, bf16[16,32,1024]{2,1,0:T(8,128)(2,1)}, u32[]{:S(2)}, u32[]{:S(2)}) collective-permute-start(bf16[16,32,1024]{2,1,0:T(8,128)(2,1)S(1)} %all-to-all-done.mine_any), channel_id=1, source_target_pairs={{0,1},{1,0},{2,3},{3,2},{4,5},{5,4},{6,7},{7,6},{8,9},{9,8},{10,11... | collective-permute-start | bytes 3145736 | tf_op jit(solution)/shard_map/ppermute | solution.py:204
  30.3 8.2 %collective-permute-start.2 = (bf16[2,64,512]{2,1,0:T(8,128)(2,1)S(1)}, bf16[2,64,512]{2,1,0:T(8,128)(2,1)S(1)}, u32[]{:S(2)}, u32[]{:S(2)}) collective-permute-start(bf16[2,64,512]{2,1,0:T(8,128)(2,1)S(1)} %pad_maximum_fusion.2), channel_id=1, source_target_pairs={{0,96},{32,64},{64,32},{96,0},{128,224},{160,192},{192,160},{224,1... | collective-permute-start | bytes 393224 | tf_op jit(solution)/shard_map/ppermute | solution.py:208
  38.5 18.3 %collective-permute-start.3 = (bf16[4,64,512]{2,1,0:T(8,128)(2,1)S(1)}, bf16[4,64,512]{2,1,0:T(8,128)(2,1)S(1)}, u32[]{:S(2)}, u32[]{:S(2)}) collective-permute-start(bf16[4,64,512]{2,1,0:T(8,128)(2,1)S(1)} %pad_maximum_fusion.1), channel_id=1, source_target_pairs={{0,128},{32,160},{64,192},{96,224},{128,0},{160,32},{192,64},{224,... | collective-permute-start | bytes 786440 | tf_op jit(solution)/shard_map/ppermute | solution.py:208
  41.3 47.5 %all-to-all-start.1 = ((bf16[16,32,512]{2,1,0:T(8,128)(2,1)}), bf16[16,32,512]{2,1,0:T(8,128)(2,1)S(1)}, u32[]{:S(2)}, u32[]{:S(2)}) async-start(bf16[16,32,512]{2,1,0:T(8,128)(2,1)} %broadcast_in_dim.29), calls=%async_computation.1 | async-start | bytes 1048576 | tf_op jit(solution)/shard_map/all_to_all | solution.py:200
  56.9 31.9 %copy-start.2 = (bf16[8,64,512]{2,1,0:T(8,128)(2,1)}, bf16[8,64,512]{2,1,0:T(8,128)(2,1)S(1)}, u32[]{:S(2)}) copy-start(bf16[8,64,512]{2,1,0:T(8,128)(2,1)S(1)} %pad_maximum_fusion.cfirst) | copy-start | bytes 1572868
  56.9 31.9 %collective-permute-start.4 = (bf16[8,64,512]{2,1,0:T(8,128)(2,1)S(1)}, bf16[8,64,512]{2,1,0:T(8,128)(2,1)S(1)}, u32[]{:S(2)}, u32[]{:S(2)}) collective-permute-start(bf16[8,64,512]{2,1,0:T(8,128)(2,1)S(1)} %pad_maximum_fusion.cfirst), channel_id=1, source_target_pairs={{0,384},{32,416},{64,448},{96,480},{128,256},{160,288},{192,320},{... | collective-permute-start | bytes 1572872 | tf_op jit(solution)/shard_map/ppermute | solution.py:208
  88.8 6.4 %copy-start.1 = (bf16[16,32,512]{2,1,0:T(8,128)(2,1)}, bf16[16,32,512]{2,1,0:T(8,128)(2,1)S(1)}, u32[]{:S(2)}) copy-start(bf16[16,32,512]{2,1,0:T(8,128)(2,1)S(1)} %all-to-all-done.1.rmine) | copy-start | bytes 1572868
  88.8 6.4 %copy-start.4 = (bf16[8,64,512]{2,1,0:T(8,128)(2,1)}, bf16[8,64,512]{2,1,0:T(8,128)(2,1)S(1)}, u32[]{:S(2)}) copy-start(bf16[8,64,512]{2,1,0:T(8,128)(2,1)S(1)} %collective-permute-done.4.clast) | copy-start | bytes 1572868
  88.9 6.4 %collective-permute-start.5 = (bf16[16,32,512]{2,1,0:T(8,128)(2,1)S(1)}, bf16[16,32,512]{2,1,0:T(8,128)(2,1)S(1)}, u32[]{:S(2)}, u32[]{:S(2)}) collective-permute-start(bf16[16,32,512]{2,1,0:T(8,128)(2,1)S(1)} %all-to-all-done.1.rmine), channel_id=1, source_target_pairs={{0,1},{1,0},{2,3},{3,2},{4,5},{5,4},{6,7},{7,6},{8,9},{9,8},{10,11... | collective-permute-start | bytes 1572872 | tf_op jit(solution)/shard_map/ppermute | solution.py:204
  95.2 0.8 copy-start.5
